TPU v7x, 1024 devices: a whole 4x8x16 slice. The times are simulated.
1024 devices in a mesh: aux: 16 (over z), row: 8 (over x, core), col: 8 (over y).
Axes of the slice: x: 4, y: 8, z: 16, core: 2. Of those that a mesh axis runs over, the one named last changes fastest.
Arguments:
- three_index: bfloat16 [10240, 3, 4608], P(('aux', 'row')), may hold values from -0.59765625 to 0.59765625
- vir_coef: bfloat16 [4608, 4096], P(None, 'col'), may hold values from -0.09375 to 0.09375
- owner_count: int32 [128], P(('aux', 'row')), may hold values from 20 to 80, as said below
- pair_index: int32 [2, 2], replicated, may hold values from 0 to 2, as said below
- occ_energy: float32 [3], replicated, may hold values from -2 to -0.6
- vir_energy: float32 [4096], replicated, may hold values from 0.3 to 3
Outputs:
- aux_density: float32 [10240, 2, 4096], P(('aux', 'row'), None, 'col')
Inputs may be any that keep to these rules, and one draw needn't show every extreme that they name: `owner_count`: each owner holds between 20 and 80 live functions; both ends are reached in every draw. `pair_index`: i and j of a pair differ; every occupied orbital of the window appears.
All inputs are finite; a program needn't handle non-finite values.
Results may differ from a plain program's by a relative error of at most 0.022.
Values may be sent and summed in bfloat16 or wider, within the bound.
No kernel may reach another device: no remote copies, remote signals or barrier semaphores. Data moves between devices by JAX's collectives and lax.ppermute only.
A program may use at most 64 MiB of HBM per device.

v0:
```python
import jax
import jax.numpy as jnp
from jax import lax
from jax.sharding import PartitionSpec as P


def from_root(shard, axis, root):
    mine = lax.axis_index(axis) == root
    return lax.psum(jnp.where(mine, shard, jnp.zeros_like(shard)), axis)


def local(three_index, vir_coef, owner_count, pair_index, occ_energy, vir_energy):
    slot_total = three_index.shape[0]
    occ_width = three_index.shape[1]
    basis_width = three_index.shape[2]
    col_width = vir_coef.shape[1]
    pair_total = pair_index.shape[0]
    vir_total = vir_energy.shape[0]
    row_count = lax.axis_size("row")
    col_count = lax.axis_size("col")
    row_width = vir_total // row_count
    row_index = lax.axis_index("row")
    col_index = lax.axis_index("col")
    flat_rows = three_index.reshape(slot_total * occ_width, basis_width)
    transformed = jnp.dot(flat_rows, vir_coef, preferred_element_type=jnp.float32)
    transformed = transformed.reshape(slot_total, occ_width, col_width)
    is_live = jnp.arange(slot_total, dtype=jnp.int32) < owner_count[0]
    local_rows = jnp.where(is_live[:, None, None], transformed, jnp.zeros_like(transformed)).astype(
        jnp.bfloat16
    )
    chosen = jnp.concatenate([pair_index[:, 0], pair_index[:, 1]])
    picker_mask = chosen[:, None] == jnp.arange(occ_width, dtype=jnp.int32)[None, :]
    picker = picker_mask.astype(jnp.bfloat16)
    picked = jnp.einsum(
        "skc,qk->sqc",
        lax.all_gather(local_rows, "row", axis=0, tiled=True),
        picker,
        preferred_element_type=jnp.float32,
    )
    selected = picked.astype(jnp.bfloat16)
    first_all = selected[:, :pair_total, :]
    second_rows = selected[:, pair_total:, :]
    root_col = row_index * col_count // row_count
    first_rows = from_root(first_all, "col", root_col)
    partial_value = jnp.einsum(
        "sqa,sqb->qab", first_rows, second_rows, preferred_element_type=jnp.float32
    )
    energies = jnp.sum(picker_mask.astype(jnp.float32) * occ_energy[None, :], axis=1)
    pair_energy = energies[:pair_total] + energies[pair_total:]
    first_vir = lax.dynamic_slice_in_dim(vir_energy, row_index * row_width, row_width)
    second_vir = lax.dynamic_slice_in_dim(vir_energy, col_index * col_width, col_width)
    denominator = pair_energy[:, None, None] - first_vir[None, :, None] - second_vir[None, None, :]
    sum_share = lax.psum_scatter(
        partial_value.reshape(-1).astype(jnp.bfloat16), "aux", scatter_dimension=0, tiled=True
    ).astype(jnp.float32)
    share_length = sum_share.shape[0]
    denom_share = lax.dynamic_slice_in_dim(
        denominator.reshape(-1), lax.axis_index("aux") * share_length, share_length
    )
    amp_share = (sum_share / denom_share).astype(jnp.bfloat16)
    amplitude = lax.all_gather(amp_share, "aux", axis=0, tiled=True).reshape(partial_value.shape)
    return lax.psum_scatter(
        jnp.einsum(
            "sqa,qab->sqb", first_rows, amplitude, preferred_element_type=jnp.float32
        ).astype(jnp.bfloat16),
        "row",
        scatter_dimension=0,
        tiled=True,
    ).astype(jnp.float32)


def solution(mesh):
    return jax.shard_map(
        local,
        mesh=mesh,
        in_specs=(P(("aux", "row"), None, None), P(None, "col"), P(("aux", "row")), P(), P(), P()),
        out_specs=P(("aux", "row"), None, "col"),
        check_vma=False,
    )
```

profile of v0, /device:TPU:1, one launch (start us, length us, event | category | flops | bytes accessed | tf_op | source)
XLA Modules:
  0.0 478.1 jit_solution(8346026820360923231)
XLA Ops:
  6.5 0.0 copy-start
  6.5 0.0 all-gather.3.cloned.1.call-start
  7.4 0.8 copy-done
  8.2 0.0 copy-start.1
  8.2 4.3 fusion.11
  12.5 0.0 all-gather.3.cloned.1.call-update
  12.5 0.0 all-reduce.6.cloned.1.call-start
  12.6 0.0 copy-done.1
  12.6 0.2 slice_reduce_fusion.1
  12.8 0.1 pad_add_fusion
  12.9 44.5 %all-gather.3.cloned.1.call-done = bf16[640,3,512]{2,0,1:T(8,128)(2,1)} async-done(((bf16[80,3,512]{2,0,1:T(8,128)(2,1)}), bf16[640,3,512]{2,0,1:T(8,128)(2,1)}) %all-gather.3.cloned.1.call-update) | async-done | bytes 1966096 | tf_op jit(solution)/shard_map/all_gather | solution.py:36
  57.3 3.4 convert_bitcast_fusion
  60.7 3.2 broadcast_select_fusion
  64.0 0.0 all-reduce.6.cloned.1.call-update
  64.0 0.0 all-reduce.8.cloned.1.call-start
  64.0 90.3 %all-reduce.6.cloned.1.call-done = bf16[640,2,512]{2,1,0:T(2,128)(2,1)} async-done(((bf16[640,2,512]{2,1,0:T(2,128)(2,1)}), bf16[640,2,512]{2,1,0:T(2,128)(2,1)}) %all-reduce.6.cloned.1.call-update) | async-done | bytes 1310736 | tf_op jit(solution)/shard_map/psum | solution.py:9
  154.4 2.3 convolution_convert_fusion.1
  156.7 0.0 copy-start.2
  156.7 1.4 copy.23
  158.1 0.0 all-reduce.8.cloned.1.call-update
  158.2 0.0 all-gather.5.cloned.1.call-start
  158.2 0.8 fusion.19
  159.1 0.0 copy-done.2
  159.1 0.2 select_reduce_fusion
  159.3 0.1 slice_add_fusion
  159.3 0.1 broadcast_subtract_fusion.1
  159.4 0.2 broadcast_subtract_fusion
  159.6 1.9 copy.24
  161.5 1.3 dynamic-slice
  163.4 133.8 %all-reduce.8.cloned.1.call-done = bf16[524288]{0:T(1024)(128)(2,1)} async-done(((bf16[524288]{0:T(1024)(128)(2,1)}), bf16[524288]{0:T(1024)(128)(2,1)}) %all-reduce.8.cloned.1.call-update) | async-done | bytes 1048592
  297.2 1.6 divide_convert_fusion
  298.7 0.0 all-gather.5.cloned.1.call-update
  298.8 0.0 all-reduce.10.cloned.1.call-start
  298.8 72.3 %all-gather.5.cloned.1.call-done = bf16[524288]{0:T(1024)(128)(2,1)} async-done(((bf16[32768]{0:T(1024)(128)(2,1)}), bf16[524288]{0:T(1024)(128)(2,1)}) %all-gather.5.cloned.1.call-update) | async-done | bytes 1048592 | tf_op jit(solution)/shard_map/all_gather | solution.py:61
  371.1 2.5 reshape.52
  373.5 2.8 fusion.6
  376.4 2.8 copy.21
  379.2 0.0 all-reduce.10.cloned.1.call-update
  379.2 1.3 dynamic-slice.2
  381.1 88.7 %all-reduce.10.cloned.1.call-done = bf16[640,2,512]{2,1,0:T(2,128)(2,1)} async-done(((bf16[640,2,512]{2,1,0:T(2,128)(2,1)}), bf16[640,2,512]{2,1,0:T(2,128)(2,1)}) %all-reduce.10.cloned.1.call-update) | async-done | bytes 1310736
  469.8 1.8 dynamic-slice_convert_fusion
  (1 shorter events, 0.0 us)
Async XLA Ops:
  6.5 1.6 copy-start
  6.5 50.8 %all-gather.3.cloned.1.call-start = ((), (), s32[]{:S(2)}) async-start(), calls=%async_computation | async-start | bytes 2211840 | tf_op jit(solution)/shard_map/all_gather | solution.py:36
  8.2 4.4 copy-start.1
  12.5 141.8 %all-reduce.6.cloned.1.call-start = ((), (), s32[]{:S(2)}) async-start(), calls=%async_computation.1 | async-start | bytes 2621440 | tf_op jit(solution)/shard_map/psum | solution.py:9
  64.0 233.2 %all-reduce.8.cloned.1.call-start = ((), (), s32[]{:S(2)}) async-start(), calls=%async_computation.3 | async-start | bytes 2097152
  156.7 2.3 copy-start.2
  158.2 212.9 %all-gather.5.cloned.1.call-start = ((), (), s32[]{:S(2)}) async-start(), calls=%async_computation.2 | async-start | bytes 1114112 | tf_op jit(solution)/shard_map/all_gather | solution.py:61
  298.8 171.1 %all-reduce.10.cloned.1.call-start = ((), (), s32[]{:S(2)}) async-start(), calls=%async_computation.4 | async-start | bytes 2621440
Sparse Core Ops, SparseCore 0:
  12.7 44.6 all-gather.2
  64.1 90.2 all-reduce.5
  158.3 138.8 all-reduce.7
  300.1 70.9 all-gather.4
  379.3 90.4 all-reduce.9
where the time goes:
time: 479 us; the launch traced here: 478 us
  waiting for transfers between devices  430 us (90%)
  between operations  15.3 us (3%)
  local copies, waits for them, and re-layouts  12.9 us (3%)
  matrix products  12.9 us (3%)
  other arithmetic  7.15 us (1%)
    unnamed x7, waiting for transfers between devices  223 us
    psum x1, waiting for transfers between devices, from_root(): return lax.psum(jnp.where(mine, shard, jnp.zeros_like(shard)), axis)  90.3 us
    all_gather x1, waiting for transfers between devices, local(): lax.all_gather(amp_share, 'aux', axis=0, tiled=True)  72.3 us
    all_gather x1, waiting for transfers between devices, local(): lax.all_gather(local_rows, 'row', axis=0, tiled=True)  44.5 us
  transfers between devices with their start and end apart: 5, of which 5 were waited for; matrix products, arithmetic and copies ran while one was open for 1% of the time, Pallas kernels for 0%

commit v1 on v0

v1 whole, which is shorter than its diff:
```python
import jax
import jax.numpy as jnp
from jax import lax
from jax.experimental import pallas as pl
from jax.experimental.pallas import tpu as pltpu
from jax.sharding import Mesh, PartitionSpec as P

VMEM_LIMIT = 48 * 1024 * 1024
f32, bf16 = jnp.float32, jnp.bfloat16

NAMES = ("zh", "zl", "x", "k", "y")
S1, S2 = "x", "zh"
GM = "zl"


def params():
    return pltpu.CompilerParams(vmem_limit_bytes=VMEM_LIMIT)


def transform(rows, coef, count, pairs):
    occ, slots, basis = rows.shape
    width = coef.shape[1]
    pair_total = pairs.shape[0]
    step = 512
    steps = basis // step

    def kernel(count_ref, pairs_ref, rows_ref, coef_ref, first_ref, second_ref, total, held):
        at = pl.program_id(0)

        @pl.when(at == 0)
        def _():
            total[...] = jnp.zeros_like(total)

        total[...] += jnp.dot(
            rows_ref[...].reshape(occ * slots, step), coef_ref[...], preferred_element_type=f32
        )

        @pl.when(at == steps - 1)
        def _():
            value = total[...].reshape(occ, slots, width)
            place = lax.broadcasted_iota(jnp.int32, (occ, slots, width), 1)
            held[...] = jnp.where(place < count_ref[0], value, 0.0).astype(bf16)
            for q in range(pair_total):
                first_ref[q] = held[pairs_ref[q, 0]]
                second_ref[q] = held[pairs_ref[q, 1]]

    out = jax.ShapeDtypeStruct((pair_total, slots, width), bf16)
    whole = pl.BlockSpec((pair_total, slots, width), lambda i: (0, 0, 0))
    return pl.pallas_call(
        kernel,
        grid=(steps,),
        in_specs=[
            pl.BlockSpec(memory_space=pltpu.SMEM),
            pl.BlockSpec(memory_space=pltpu.SMEM),
            pl.BlockSpec((occ, slots, step), lambda i: (0, 0, i)),
            pl.BlockSpec((step, width), lambda i: (i, 0)),
        ],
        out_specs=[whole, whole],
        out_shape=[out, out],
        scratch_shapes=[
            pltpu.VMEM((occ * slots, width), f32),
            pltpu.VMEM((occ, slots, width), bf16),
        ],
        compiler_params=params(),
    )(count, pairs, rows, coef)


def coulomb_parts(first, second, n1, n2):
    owners, pair_total, slots, width = first.shape
    piece = width // (n1 * n2)

    def kernel(first_ref, second_ref, out_ref):
        a = first_ref[...].reshape(owners * slots, width)
        b = second_ref[...].reshape(owners * slots, width)
        value = lax.dot_general(a, b, (((0,), (0,)), ((), ())), preferred_element_type=f32)
        out_ref[...] = value.astype(bf16).reshape(n1, n2, 1, piece, width)

    block = pl.BlockSpec((owners, 1, slots, width), lambda q: (0, q, 0, 0))
    return pl.pallas_call(
        kernel,
        grid=(pair_total,),
        in_specs=[block, block],
        out_specs=pl.BlockSpec((n1, n2, 1, piece, width), lambda q: (0, 0, q, 0, 0)),
        out_shape=jax.ShapeDtypeStruct((n1, n2, pair_total, piece, width), bf16),
        compiler_params=params(),
    )(first, second)


def density_parts(first, amplitude, gm, cores):
    owners, pair_total, slots, width = first.shape
    n1, n2, _, piece, _ = amplitude.shape

    def kernel(first_ref, amp_ref, out_ref):
        a = first_ref[...].reshape(owners * slots, width)
        b = amp_ref[...].reshape(n1 * n2 * piece, width)
        value = jnp.dot(a, b, preferred_element_type=f32).astype(bf16)
        value = value.reshape(gm, cores, slots, width)
        for k in range(cores):
            for m in range(gm):
                out_ref[k, m, 0] = value[m, k]

    return pl.pallas_call(
        kernel,
        grid=(pair_total,),
        in_specs=[
            pl.BlockSpec((owners, 1, slots, width), lambda q: (0, q, 0, 0)),
            pl.BlockSpec((n1, n2, 1, piece, width), lambda q: (0, 0, q, 0, 0)),
        ],
        out_specs=pl.BlockSpec((cores, gm, 1, slots, width), lambda q: (0, 0, q, 0, 0)),
        out_shape=jax.ShapeDtypeStruct((cores, gm, pair_total, slots, width), bf16),
        compiler_params=params(),
    )(first, amplitude)


def added(parts):
    total = parts[0].astype(f32)
    for k in range(1, parts.shape[0]):
        total = total + parts[k].astype(f32)
    return total


def exchange(parts, axis):
    return lax.all_to_all(parts, axis, 0, 0, tiled=True)


def spread(part, axis):
    copies = jnp.broadcast_to(part[None], (lax.axis_size(axis),) + part.shape)
    return exchange(lax.optimization_barrier(copies), axis)


def make_local(sizes):
    gm, cores, cols = sizes[GM], sizes["k"], sizes["y"]
    n1, n2 = sizes[S1], sizes[S2]
    order = (GM, "k", "y")
    swap = []
    for m in range(gm):
        for k in range(cores):
            for y in range(cols):
                swap.append(((m * cores + k) * cols + y, y * cols + (m * cores + k)))

    def local(three_index, vir_coef, owner_count, pair_index, occ_energy, vir_energy):
        slots, occ, _ = three_index.shape
        width = vir_coef.shape[1]
        pair_total = pair_index.shape[0]
        rows = jnp.transpose(three_index, (1, 0, 2))
        first, second = transform(rows, vir_coef, owner_count, pair_index)
        second_all = lax.all_gather(second, (GM, "k"), axis=0, tiled=False)
        second_all = second_all.reshape((gm * cores,) + second.shape)
        first_turned = lax.ppermute(first, order, swap)
        first_all = spread(first_turned, "y")
        parts = coulomb_parts(first_all, second_all, n1, n2)
        mine = added(exchange(parts, S1)).astype(bf16)
        share = added(exchange(mine, S2))
        piece = width // (n1 * n2)
        block = lax.axis_index(GM) * cores + lax.axis_index("k")
        start = block * width + lax.axis_index(S1) * (width // n1) + lax.axis_index(S2) * piece
        first_vir = lax.dynamic_slice_in_dim(vir_energy, start, piece)
        second_vir = lax.dynamic_slice_in_dim(vir_energy, lax.axis_index("y") * width, width)
        mask = pair_index[:, :, None] == jnp.arange(occ, dtype=jnp.int32)
        pair_energy = jnp.sum(jnp.where(mask, occ_energy, 0.0), axis=(1, 2))
        denominator = pair_energy[:, None, None] - first_vir[:, None] - second_vir
        amp = (share / denominator).astype(bf16)
        amp_all = spread(spread(amp, S2), S1)
        dens = density_parts(first_all, amp_all, gm, cores)
        dens = added(exchange(dens, "k")).astype(bf16)
        out = added(exchange(dens, GM))
        return jnp.transpose(out, (1, 0, 2))

    return local


def solution(mesh):
    aux, row, col = (mesh.shape[name] for name in ("aux", "row", "col"))
    sizes = {"zl": 4, "zh": aux // 4, "k": 2, "x": row // 2, "y": col}
    fine = Mesh(mesh.devices.reshape([sizes[name] for name in NAMES]), NAMES)
    owners = ("zh", "zl", "x", "k")
    return jax.shard_map(
        make_local(sizes),
        mesh=fine,
        in_specs=(P(owners, None, None), P(None, "y"), P(owners), P(), P(), P()),
        out_specs=P(owners, None, "y"),
        check_vma=False,
    )
```

time: 479 us -> 207 us (0.43)
  waiting for transfers between devices: 430 us -> 51.1 us
  blocking collectives: 0 us -> 80 us
  starting transfers between devices: 0.17 us -> 41.8 us
  matrix products: 12.9 us -> 0 us
  Pallas kernels: 0 us -> 10.4 us
  other arithmetic: 7.15 us -> 1.44 us
  local copies, waits for them, and re-layouts: 12.9 us -> 7.43 us
    unnamed x7 -> x1, waiting for transfers between devices: 223 us -> 0.02 us
    psum x1 -> x0, waiting for transfers between devices: 90.3 us -> none  [from_root(): return lax.psum(jnp.where(mine, shard, jnp.zeros_like(shard)), axis)]
    all_gather x2 -> x1, waiting for transfers between devices: 117 us -> 30.4 us  [local(): second_all = lax.all_gather(second, (GM, 'k'), axis=0, tiled=False)]
    all_to_all x0 -> x5, blocking collectives: none -> 80 us  [exchange(): return lax.all_to_all(parts, axis, 0, 0, tiled=True)]
    all_to_all x0 -> x2, starting transfers between devices: none -> 37.2 us  [exchange(): return lax.all_to_all(parts, axis, 0, 0, tiled=True)]
    all_to_all x0 -> x2, waiting for transfers between devices: none -> 17.7 us  [exchange(): return lax.all_to_all(parts, axis, 0, 0, tiled=True)]
    dot_general x4 -> x0, matrix products: 12.9 us -> none  [the longest x1 4.35 us: local(): jnp.dot(flat_rows, vir_coef, preferred_element_type=jnp.float32)]
    pallas_call x0 -> x3, Pallas kernels: none -> 10.4 us  [the longest x1 7.67 us: transform(): pl.pallas_call(kernel, grid=(steps,), in_specs=[pl.BlockSpec(memory_space...]
  transfers between devices with their start and end apart: 5 -> 4, of which waited for: 5 -> 4; matrix products, arithmetic and copies ran while one was open for 1% -> 1% of each run, Pallas kernels for 0% -> 0%
where the time goes in v1:
time: 207 us; the launch traced here: 206 us
  blocking collectives  80 us (39%)
  waiting for transfers between devices  51.1 us (25%)
  starting transfers between devices  41.8 us (20%)
  between operations  14.1 us (7%)
  Pallas kernels  10.4 us (5%)
  local copies, waits for them, and re-layouts  7.43 us (4%)
    all_to_all x5, blocking collectives, exchange(): return lax.all_to_all(parts, axis, 0, 0, tiled=True)  80 us
    all_to_all x2, starting transfers between devices, exchange(): return lax.all_to_all(parts, axis, 0, 0, tiled=True)  37.2 us
    all_gather x1, waiting for transfers between devices, local(): second_all = lax.all_gather(second, (GM, 'k'), axis=0, tiled=False)  30.4 us
    all_to_all x2, waiting for transfers between devices, exchange(): return lax.all_to_all(parts, axis, 0, 0, tiled=True)  17.7 us
    pallas_call x1, Pallas kernels, transform(): pl.pallas_call(kernel, grid=(steps,), in_specs=[pl.BlockSpec(memory_space...  7.67 us
    ppermute x1, starting transfers between devices, local(): first_turned = lax.ppermute(first, order, swap)  4.58 us
  transfers between devices with their start and end apart: 4, of which 4 were waited for; matrix products, arithmetic and copies ran while one was open for 1% of the time, Pallas kernels for 0%

profile of v1, /device:TPU:1, one launch (start us, length us, event | category | flops | bytes accessed | tf_op | source)
XLA Modules:
  0.0 206.2 jit_solution(15748329321144754177)
XLA Ops:
  6.5 0.0 all-gather.3.cloned.1.call-start
  7.2 0.0 copy-start
  7.2 1.6 copy-done
  8.8 0.0 copy-start.2
  8.8 0.7 copy-done.2
  9.5 7.7 %shard_map.64 = (bf16[2,80,512]{2,1,0:T(8,128)(2,1)S(1)}, bf16[2,80,512]{2,1,0:T(8,128)(2,1)}) custom-call(s32[1]{0:T(128)S(6)} %copy.10.count_ref, s32[2,2]{1,0:T(2,128)S(1)} %copy-done.2, bf16[3,80,4608]{2,1,0:T(8,128)(2,1)S(1)} %bitcast.12, bf16[4608,512]{1,0:T(8,128)(2,1)} %coef_ref.1), custom_call_target="tpu_custom_call" | custom-call | tf_op jit(solution)/shard_map/pallas_call | solution.py:49
  17.2 4.6 %collective-permute-start = (bf16[2,80,512]{2,1,0:T(8,128)(2,1)S(1)}, bf16[2,80,512]{2,1,0:T(8,128)(2,1)S(1)}, u32[]{:S(2)}, u32[]{:S(2)}) collective-permute-start(bf16[2,80,512]{2,1,0:T(8,128)(2,1)S(1)} %get-tuple-element.7), channel_id=1, source_target_pairs={{0,0},{1,8},{2,64},{3,72},{4,128},{5,136},{6,192},{7,200},{8,1},{9... | collective-permute-start | bytes 491528 | tf_op jit(solution)/shard_map/ppermute | solution.py:149
  21.8 0.0 all-gather.3.cloned.1.call-update
  21.8 3.0 %collective-permute-done = bf16[2,80,512]{2,1,0:T(8,128)(2,1)S(1)} collective-permute-done((bf16[2,80,512]{2,1,0:T(8,128)(2,1)S(1)}, bf16[2,80,512]{2,1,0:T(8,128)(2,1)S(1)}, u32[]{:S(2)}, u32[]{:S(2)}) %collective-permute-start) | collective-permute-done | bytes 163872 | tf_op jit(solution)/shard_map/ppermute | solution.py:149
  24.7 1.2 broadcast_in_dim.16
  25.9 18.8 %all-to-all-start = ((bf16[8,2,80,512]{3,2,1,0:T(8,128)(2,1)}), bf16[8,2,80,512]{3,2,1,0:T(8,128)(2,1)S(1)}, u32[]{:S(2)}, u32[]{:S(2)}) async-start(bf16[8,2,80,512]{3,2,1,0:T(8,128)(2,1)} %broadcast_in_dim.16), calls=%async_computation | async-start | bytes 2621440 | tf_op jit(solution)/shard_map/all_to_all | solution.py:123
  44.7 30.4 %all-gather.3.cloned.1.call-done = bf16[16,80,512]{2,1,0:T(8,128)(2,1)} async-done(((bf16[2,80,512]{2,1,0:T(8,128)(2,1)}), bf16[16,80,512]{2,1,0:T(8,128)(2,1)}) %all-gather.3.cloned.1.call-update) | async-done | bytes 1310736 | tf_op jit(solution)/shard_map/all_gather | solution.py:147
  75.1 4.4 %all-to-all-done.first_ref = bf16[8,2,80,512]{3,2,1,0:T(8,128)(2,1)S(1)} async-done(((bf16[8,2,80,512]{3,2,1,0:T(8,128)(2,1)}), bf16[8,2,80,512]{3,2,1,0:T(8,128)(2,1)S(1)}, u32[]{:S(2)}, u32[]{:S(2)}) %all-to-all-start) | async-done | bytes 1310752 | tf_op jit(solution)/shard_map/all_to_all | solution.py:123
  79.5 0.0 copy-start.1
  79.5 1.3 copy-done.1
  80.8 1.5 shard_map.65
  82.3 17.9 %all_to_all.35 = bf16[4,4,2,32,512]{4,3,2,1,0:T(8,128)(2,1)S(1)} all-to-all(bf16[4,4,2,32,512]{4,3,2,1,0:T(8,128)(2,1)S(1)} %shard_map.65), channel_id=1, replica_groups=mesh['zh'=4,'zl'=4,'x'=4,'k'=2,'y'=8] {'x'}, dimensions={0} | all-to-all | bytes 2097152 | tf_op jit(solution)/shard_map/all_to_all | solution.py:123
  100.2 0.0 copy-start.3
  100.2 0.0 copy-start.4
  100.2 0.8 fusion.1
  101.1 18.4 %all-to-all-start.2 = ((bf16[4,2,32,512]{3,2,1,0:T(8,128)(2,1)}), bf16[4,2,32,512]{3,2,1,0:T(8,128)(2,1)S(1)}, u32[]{:S(2)}, u32[]{:S(2)}) async-start(bf16[4,2,32,512]{3,2,1,0:T(8,128)(2,1)} %fusion.1), calls=%async_computation.2 | async-start | bytes 524288 | tf_op jit(solution)/shard_map/all_to_all | solution.py:123
  119.5 0.8 dynamic_slice.6
  120.3 0.8 dynamic_slice.7
  121.0 0.0 copy-done.3
  121.0 0.0 copy-done.4
  121.0 0.2 fusion.3
  121.2 0.1 broadcast_subtract_fusion
  121.3 13.3 %all-to-all-done.2 = bf16[4,2,32,512]{3,2,1,0:T(8,128)(2,1)S(1)} async-done(((bf16[4,2,32,512]{3,2,1,0:T(8,128)(2,1)}), bf16[4,2,32,512]{3,2,1,0:T(8,128)(2,1)S(1)}, u32[]{:S(2)}, u32[]{:S(2)}) %all-to-all-start.2) | async-done | bytes 262176 | tf_op jit(solution)/shard_map/all_to_all | solution.py:123
  134.6 0.1 fusion.2
  134.7 17.5 %all_to_all.36 = bf16[4,2,32,512]{3,2,1,0:T(8,128)(2,1)S(1)} all-to-all(bf16[4,2,32,512]{3,2,1,0:T(8,128)(2,1)S(1)} %broadcast_in_dim.36), channel_id=1, replica_groups=mesh['zh'=4,'zl'=4,'x'=4,'k'=2,'y'=8] {'zh'}, dimensions={0} | all-to-all | bytes 524288 | tf_op jit(solution)/shard_map/all_to_all | solution.py:123
  152.2 0.1 broadcast_in_dim.37
  152.3 12.2 %all_to_all.37.amp_ref = bf16[4,4,2,32,512]{4,3,2,1,0:T(8,128)(2,1)S(1)} all-to-all(bf16[4,4,2,32,512]{4,3,2,1,0:T(8,128)(2,1)S(1)} %broadcast_in_dim.37), channel_id=1, replica_groups=mesh['zh'=4,'zl'=4,'x'=4,'k'=2,'y'=8] {'x'}, dimensions={0} | all-to-all | bytes 2097152 | tf_op jit(solution)/shard_map/all_to_all | solution.py:123
  164.5 1.3 shard_map.66
  165.8 12.7 %all_to_all.38 = bf16[2,4,2,80,512]{4,3,2,1,0:T(8,128)(2,1)S(1)} all-to-all(bf16[2,4,2,80,512]{4,3,2,1,0:T(8,128)(2,1)S(1)} %shard_map.66), channel_id=1, replica_groups=mesh['zh'=4,'zl'=4,'x'=4,'k'=2,'y'=8] {'k'}, dimensions={0} | all-to-all | bytes 2621440 | tf_op jit(solution)/shard_map/all_to_all | solution.py:123
  178.5 0.2 fusion
  178.7 19.6 %all_to_all.39 = bf16[4,2,80,512]{3,2,1,0:T(8,128)(2,1)S(1)} all-to-all(bf16[4,2,80,512]{3,2,1,0:T(8,128)(2,1)S(1)} %fusion), channel_id=1, replica_groups=mesh['zh'=4,'zl'=4,'x'=4,'k'=2,'y'=8] {'zl'}, dimensions={0} | all-to-all | bytes 1310720 | tf_op jit(solution)/shard_map/all_to_all | solution.py:123
  198.3 0.1 add_bitcast_fusion
  198.4 1.0 copy.9
  (1 shorter events, 0.0 us)
Async XLA Ops:
  6.5 68.6 %all-gather.3.cloned.1.call-start = ((), (), s32[]{:S(2)}) async-start(), calls=%async_computation.7 | async-start | bytes 1474560 | tf_op jit(solution)/shard_map/all_gather | solution.py:147
  7.2 1.6 copy-start
  8.8 0.7 copy-start.2
  17.2 7.6 %collective-permute-start = (bf16[2,80,512]{2,1,0:T(8,128)(2,1)S(1)}, bf16[2,80,512]{2,1,0:T(8,128)(2,1)S(1)}, u32[]{:S(2)}, u32[]{:S(2)}) collective-permute-start(bf16[2,80,512]{2,1,0:T(8,128)(2,1)S(1)} %get-tuple-element.7), channel_id=1, source_target_pairs={{0,0},{1,8},{2,64},{3,72},{4,128},{5,136},{6,192},{7,200},{8,1},{9... | collective-permute-start | bytes 491528 | tf_op jit(solution)/shard_map/ppermute | solution.py:149
  25.9 53.6 %all-to-all-start = ((bf16[8,2,80,512]{3,2,1,0:T(8,128)(2,1)}), bf16[8,2,80,512]{3,2,1,0:T(8,128)(2,1)S(1)}, u32[]{:S(2)}, u32[]{:S(2)}) async-start(bf16[8,2,80,512]{3,2,1,0:T(8,128)(2,1)} %broadcast_in_dim.16), calls=%async_computation | async-start | bytes 2621440 | tf_op jit(solution)/shard_map/all_to_all | solution.py:123
  79.5 1.3 copy-start.1
  100.2 20.8 %copy-start.3 = (s32[2,2]{1,0:T(2,128)S(1)}, s32[2,2]{1,0:T(2,128)}, u32[]{:S(2)}) copy-start(s32[2,2]{1,0:T(2,128)} %pairs_ref.1) | copy-start | bytes 52
  100.2 20.8 %copy-start.4 = (f32[3]{0:T(128)S(1)}, f32[3]{0:T(128)}, u32[]{:S(2)}) copy-start(f32[3]{0:T(128)} %param.10) | copy-start | bytes 40
  101.1 33.5 %all-to-all-start.2 = ((bf16[4,2,32,512]{3,2,1,0:T(8,128)(2,1)}), bf16[4,2,32,512]{3,2,1,0:T(8,128)(2,1)S(1)}, u32[]{:S(2)}, u32[]{:S(2)}) async-start(bf16[4,2,32,512]{3,2,1,0:T(8,128)(2,1)} %fusion.1), calls=%async_computation.2 | async-start | bytes 524288 | tf_op jit(solution)/shard_map/all_to_all | solution.py:123
Sparse Core Ops, SparseCore 0:
  21.9 53.1 all-gather.2

commit v2 on v1

v2 whole, which is shorter than its diff:
```python
import jax
import jax.numpy as jnp
from jax import lax
from jax.experimental import pallas as pl
from jax.experimental.pallas import tpu as pltpu
from jax.sharding import Mesh, PartitionSpec as P

VMEM_LIMIT = 48 * 1024 * 1024
f32, bf16 = jnp.float32, jnp.bfloat16

NAMES = ("zh", "zl", "x", "k", "y")
S1, S2 = "x", "zh"
GM = "zl"


def params():
    return pltpu.CompilerParams(vmem_limit_bytes=VMEM_LIMIT)


def transform(rows, coef, count, pairs):
    occ, slots, basis = rows.shape
    width = coef.shape[1]
    pair_total = pairs.shape[0]
    step = 512
    steps = basis // step

    def kernel(count_ref, pairs_ref, rows_ref, coef_ref, first_ref, second_ref, coefs, held, sems):
        copies = [
            pltpu.make_async_copy(coef_ref.at[pl.ds(k * step, step)], coefs.at[k], sems.at[k])
            for k in range(steps)
        ]
        for copy in copies:
            copy.start()
        total = jnp.zeros((occ * slots, width), f32)
        for k in range(steps):
            copies[k].wait()
            part = rows_ref[:, :, k * step : (k + 1) * step].reshape(occ * slots, step)
            total += jnp.dot(part, coefs[k], preferred_element_type=f32)
        value = total.reshape(occ, slots, width)
        place = lax.broadcasted_iota(jnp.int32, (occ, slots, width), 1)
        held[...] = jnp.where(place < count_ref[0], value, 0.0).astype(bf16)
        for q in range(pair_total):
            first_ref[q] = held[pairs_ref[q, 0]]
            second_ref[q] = held[pairs_ref[q, 1]]

    out = jax.ShapeDtypeStruct((pair_total, slots, width), bf16)
    smem = pl.BlockSpec(memory_space=pltpu.SMEM)
    vmem = pl.BlockSpec(memory_space=pltpu.VMEM)
    return pl.pallas_call(
        kernel,
        in_specs=[smem, smem, vmem, pl.BlockSpec(memory_space=pl.ANY)],
        out_specs=[vmem, vmem],
        out_shape=[out, out],
        scratch_shapes=[
            pltpu.VMEM((steps, step, width), bf16),
            pltpu.VMEM((occ, slots, width), bf16),
            pltpu.SemaphoreType.DMA((steps,)),
        ],
        compiler_params=params(),
    )(count, pairs, rows, coef)


def coulomb_parts(first, second, n1, n2):
    groups, cores, pair_total, slots, width = first.shape
    piece = width // (n1 * n2)
    depth = groups * slots

    def kernel(first_ref, *refs):
        out_ref = refs[-1]
        value = jnp.zeros((width, width), f32)
        for k in range(cores):
            a = first_ref[:, k, 0].reshape(depth, width)
            b = refs[k][...].reshape(depth, width)
            value += lax.dot_general(a, b, (((0,), (0,)), ((), ())), preferred_element_type=f32)
        out_ref[...] = value.astype(bf16).reshape(n1, n2, 1, piece, width)

    return pl.pallas_call(
        kernel,
        grid=(pair_total,),
        in_specs=[pl.BlockSpec((groups, cores, 1, slots, width), lambda q: (0, 0, q, 0, 0))]
        + [pl.BlockSpec((groups, 1, slots, width), lambda q: (0, q, 0, 0))] * cores,
        out_specs=pl.BlockSpec((n1, n2, 1, piece, width), lambda q: (0, 0, q, 0, 0)),
        out_shape=jax.ShapeDtypeStruct((n1, n2, pair_total, piece, width), bf16),
        compiler_params=params(),
    )(first, *second)


def density_parts(first, amplitude, targets):
    groups, cores, pair_total, slots, width = first.shape
    n1, n2, _, piece, _ = amplitude.shape

    def kernel(targets_ref, first_ref, amp_ref, *outs):
        b = amp_ref[...].reshape(n1 * n2 * piece, width)
        for k in range(cores):
            a = first_ref[:, k, 0].reshape(groups * slots, width)
            value = jnp.dot(a, b, preferred_element_type=f32).astype(bf16)
            value = value.reshape(groups, slots, width)
            for m in range(groups):
                outs[k][targets_ref[m], 0] = value[m]

    return pl.pallas_call(
        kernel,
        grid=(pair_total,),
        in_specs=[
            pl.BlockSpec(memory_space=pltpu.SMEM),
            pl.BlockSpec((groups, cores, 1, slots, width), lambda q: (0, 0, q, 0, 0)),
            pl.BlockSpec((n1, n2, 1, piece, width), lambda q: (0, 0, q, 0, 0)),
        ],
        out_specs=[pl.BlockSpec((groups, 1, slots, width), lambda q: (0, q, 0, 0))] * cores,
        out_shape=[jax.ShapeDtypeStruct((groups, pair_total, slots, width), bf16)] * cores,
        compiler_params=params(),
    )(targets, first, amplitude)


def added(parts):
    total = parts[0].astype(f32)
    for k in range(1, parts.shape[0]):
        total = total + parts[k].astype(f32)
    return total


def exchange(parts, axis):
    return lax.all_to_all(parts, axis, 0, 0, tiled=True)


def spread(part, axis):
    copies = jnp.broadcast_to(part[None], (lax.axis_size(axis),) + part.shape)
    return exchange(lax.optimization_barrier(copies), axis)


def make_local(sizes):
    gm, cores, cols = sizes[GM], sizes["k"], sizes["y"]
    n1, n2 = sizes[S1], sizes[S2]
    order = (GM, "k", "y")
    turn = []
    for m in range(gm):
        for k in range(cores):
            for y in range(cols):
                to_m, to_k = y % gm, y // gm
                to_y = (to_m - m) % gm * cores + (k ^ to_k)
                turn.append(((m * cores + k) * cols + y, (to_m * cores + to_k) * cols + to_y))
    swap = [(0, 1), (1, 0)]

    def local(three_index, vir_coef, owner_count, pair_index, occ_energy, vir_energy):
        slots, occ, _ = three_index.shape
        width = vir_coef.shape[1]
        pair_total = pair_index.shape[0]
        rows = jnp.transpose(three_index, (1, 0, 2))
        first, second = transform(rows, vir_coef, owner_count, pair_index)
        turned = lax.ppermute(first, order, turn)
        piece = width // (n1 * n2)
        block = lax.axis_index("k") * gm + lax.axis_index(GM)
        start = block * width + lax.axis_index(S1) * (width // n1) + lax.axis_index(S2) * piece
        first_vir = lax.dynamic_slice_in_dim(vir_energy, start, piece)
        second_vir = lax.dynamic_slice_in_dim(vir_energy, lax.axis_index("y") * width, width)
        mask = pair_index[:, :, None] == jnp.arange(occ, dtype=jnp.int32)
        pair_energy = jnp.sum(jnp.where(mask, occ_energy, 0.0), axis=(1, 2))
        denominator = pair_energy[:, None, None] - first_vir[:, None] - second_vir
        targets = (lax.axis_index(GM) - jnp.arange(gm, dtype=jnp.int32)) % gm
        turned, denominator, targets = lax.optimization_barrier((turned, denominator, targets))
        copies = jnp.broadcast_to(turned[None], (cols,) + turned.shape)
        copies, second = lax.optimization_barrier((copies, second))
        first_all = exchange(copies, "y").reshape((gm, cores) + first.shape)
        rings = [second]
        for d in range(1, gm):
            rings.append(lax.ppermute(second, GM, [(m, (m + d) % gm) for m in range(gm)]))
        second_own = jnp.stack(rings)
        second_other = lax.ppermute(second_own, "k", swap)
        parts = coulomb_parts(first_all, (second_own, second_other), n1, n2)
        mine = added(exchange(parts, S1)).astype(bf16)
        share = added(exchange(mine, S2))
        amp = (share / denominator).astype(bf16)
        amp_all = spread(spread(amp, S2), S1)
        own, other = density_parts(first_all, amp_all, targets)
        came = lax.ppermute(other, "k", swap)
        dens = (own.astype(f32) + came.astype(f32)).astype(bf16)
        out = added(exchange(dens, GM))
        return jnp.transpose(out, (1, 0, 2))

    return local


def solution(mesh):
    aux, row, col = (mesh.shape[name] for name in ("aux", "row", "col"))
    sizes = {"zl": 4, "zh": aux // 4, "k": 2, "x": row // 2, "y": col}
    fine = Mesh(mesh.devices.reshape([sizes[name] for name in NAMES]), NAMES)
    owners = ("zh", "zl", "x", "k")
    return jax.shard_map(
        make_local(sizes),
        mesh=fine,
        in_specs=(P(owners, None, None), P(None, "y"), P(owners), P(), P(), P()),
        out_specs=P(owners, None, "y"),
        check_vma=False,
    )
```

time: 207 us -> 190 us (0.918)
  blocking collectives: 80 us -> 107 us
  waiting for transfers between devices: 51.1 us -> 25.8 us
  between operations: 14.1 us -> 0.83 us
  Pallas kernels: 10.4 us -> 7 us
    all_gather x1 -> x0, waiting for transfers between devices: 30.4 us -> none  [local(): second_all = lax.all_gather(second, (GM, 'k'), axis=0, tiled=False)]
    all_to_all x5, blocking collectives: 80 us -> 107 us  [exchange(): return lax.all_to_all(parts, axis, 0, 0, tiled=True)]
    all_to_all x2 -> x1, starting transfers between devices: 37.2 us -> 12.1 us  [exchange(): return lax.all_to_all(parts, axis, 0, 0, tiled=True)]
    ppermute x1 -> x6, starting transfers between devices: 4.58 us -> 29.2 us  [the longest x3 12.7 us: local(): lax.ppermute(second, GM, [(m, (m + d) % gm) for m in range(gm)])]
    ppermute x1 -> x6, waiting for transfers between devices: 2.96 us -> 18.8 us  [the longest x3 10.9 us: local(): lax.ppermute(second, GM, [(m, (m + d) % gm) for m in range(gm)])]
    all_to_all x2 -> x1, waiting for transfers between devices: 17.7 us -> 7.03 us  [exchange(): return lax.all_to_all(parts, axis, 0, 0, tiled=True)]
    pallas_call x3, Pallas kernels: 10.4 us -> 7 us  [the longest x1 3.52 us: transform(): pl.pallas_call(kernel, in_specs=[smem, smem, vmem, pl.BlockSpec(memory_sp...]
  transfers between devices with their start and end apart: 4 -> 7, of which waited for: 4 -> 5; matrix products, arithmetic and copies ran while one was open for 1% -> 1% of each run, Pallas kernels for 0% -> 0%
where the time goes in v2:
time: 190 us; the launch traced here: 189 us
  blocking collectives  107 us (56%)
  starting transfers between devices  41.3 us (22%)
  waiting for transfers between devices  25.8 us (14%)
  Pallas kernels  7 us (4%)
  local copies, waits for them, and re-layouts  6.15 us (3%)
    all_to_all x5, blocking collectives, exchange(): return lax.all_to_all(parts, axis, 0, 0, tiled=True)  107 us
    ppermute x3, starting transfers between devices, local(): lax.ppermute(second, GM, [(m, (m + d) % gm) for m in range(gm)])  12.7 us
    all_to_all x1, starting transfers between devices, exchange(): return lax.all_to_all(parts, axis, 0, 0, tiled=True)  12.1 us
    ppermute x3, waiting for transfers between devices, local(): lax.ppermute(second, GM, [(m, (m + d) % gm) for m in range(gm)])  10.9 us
    ppermute x1, starting transfers between devices, local(): came = lax.ppermute(other, 'k', swap)  9.57 us
    all_to_all x1, waiting for transfers between devices, exchange(): return lax.all_to_all(parts, axis, 0, 0, tiled=True)  7.03 us
    ppermute x1, starting transfers between devices, local(): turned = lax.ppermute(first, order, turn)  4.6 us
    ppermute x1, waiting for transfers between devices, local(): turned = lax.ppermute(first, order, turn)  4.49 us
  transfers between devices with their start and end apart: 7, of which 5 were waited for; matrix products, arithmetic and copies ran while one was open for 1% of the time, Pallas kernels for 0%

profile of v2, /device:TPU:1, one launch (start us, length us, event | category | flops | bytes accessed | tf_op | source)
XLA Modules:
  0.0 189.3 jit_solution(3944429617867706354)
XLA Ops:
  0.7 0.0 copy-start
  0.7 1.6 copy-done
  2.3 0.0 copy-start.1
  2.3 0.7 copy-done.1
  3.0 0.0 copy-start.2
  3.0 0.0 copy-start.3
  3.0 3.5 %shard_map.64 = (bf16[2,80,512]{2,1,0:T(8,128)(2,1)S(1)}, bf16[2,80,512]{2,1,0:T(8,128)(2,1)S(1)}) custom-call(s32[1]{0:T(128)S(6)} %copy.9.count_ref, s32[2,2]{1,0:T(2,128)S(1)} %copy-done.1, bf16[3,80,4608]{2,1,0:T(8,128)(2,1)S(1)} %bitcast.18, bf16[4608,512]{1,0:T(8,128)(2,1)} %coef_ref.1), custom_call_target="tpu_custom_call" | custom-call | tf_op jit(solution)/shard_map/pallas_call | solution.py:49
  6.5 4.6 %collective-permute-start = (bf16[2,80,512]{2,1,0:T(8,128)(2,1)S(1)}, bf16[2,80,512]{2,1,0:T(8,128)(2,1)S(1)}, u32[]{:S(2)}, u32[]{:S(2)}) collective-permute-start(bf16[2,80,512]{2,1,0:T(8,128)(2,1)S(1)} %get-tuple-element.14), channel_id=1, source_target_pairs={{0,0},{1,66},{2,132},{3,198},{4,9},{5,75},{6,141},{7,207},{8,1},{9... | collective-permute-start | bytes 491528 | tf_op jit(solution)/shard_map/ppermute | solution.py:150
  11.1 0.0 copy-done.2
  11.1 0.0 copy-done.3
  11.1 0.2 fusion.2
  11.3 0.8 dynamic_slice.6
  12.1 0.8 dynamic_slice.7
  12.8 0.1 broadcast_subtract_fusion.1
  12.9 0.1 broadcast_subtract_fusion
  13.0 4.5 %collective-permute-done = bf16[2,80,512]{2,1,0:T(8,128)(2,1)S(1)} collective-permute-done((bf16[2,80,512]{2,1,0:T(8,128)(2,1)S(1)}, bf16[2,80,512]{2,1,0:T(8,128)(2,1)S(1)}, u32[]{:S(2)}, u32[]{:S(2)}) %collective-permute-start) | collective-permute-done | bytes 163872 | tf_op jit(solution)/shard_map/ppermute | solution.py:150
  17.5 1.2 broadcast_in_dim.16
  18.7 12.1 %all-to-all-start = ((bf16[8,2,80,512]{3,2,1,0:T(8,128)(2,1)}), bf16[8,2,80,512]{3,2,1,0:T(8,128)(2,1)S(1)}, u32[]{:S(2)}, u32[]{:S(2)}) async-start(bf16[8,2,80,512]{3,2,1,0:T(8,128)(2,1)} %broadcast_in_dim.16), calls=%async_computation | async-start | bytes 2621440 | tf_op jit(solution)/shard_map/all_to_all | solution.py:123
  30.8 8.6 %collective-permute-start.3 = (bf16[2,80,512]{2,1,0:T(8,128)(2,1)S(1)}, bf16[2,80,512]{2,1,0:T(8,128)(2,1)S(1)}, u32[]{:S(2)}, u32[]{:S(2)}) collective-permute-start(bf16[2,80,512]{2,1,0:T(8,128)(2,1)S(1)} %get-tuple-element.19), channel_id=1, source_target_pairs={{0,192},{64,0},{128,64},{192,128},{1,193},{65,1},{129,65},{193,129... | collective-permute-start | bytes 491528 | tf_op jit(solution)/shard_map/ppermute | solution.py:166
  39.4 1.9 %collective-permute-start.2 = (bf16[2,80,512]{2,1,0:T(8,128)(2,1)S(1)}, bf16[2,80,512]{2,1,0:T(8,128)(2,1)S(1)}, u32[]{:S(2)}, u32[]{:S(2)}) collective-permute-start(bf16[2,80,512]{2,1,0:T(8,128)(2,1)S(1)} %get-tuple-element.19), channel_id=1, source_target_pairs={{0,128},{64,192},{128,0},{192,64},{1,129},{65,193},{129,1},{193,65... | collective-permute-start | bytes 491528 | tf_op jit(solution)/shard_map/ppermute | solution.py:166
  41.4 2.2 %collective-permute-start.1 = (bf16[2,80,512]{2,1,0:T(8,128)(2,1)S(1)}, bf16[2,80,512]{2,1,0:T(8,128)(2,1)S(1)}, u32[]{:S(2)}, u32[]{:S(2)}) collective-permute-start(bf16[2,80,512]{2,1,0:T(8,128)(2,1)S(1)} %get-tuple-element.19), channel_id=1, source_target_pairs={{0,64},{64,128},{128,192},{192,0},{1,65},{65,129},{129,193},{193,1... | collective-permute-start | bytes 491528 | tf_op jit(solution)/shard_map/ppermute | solution.py:166
  43.6 0.0 collective-permute-done.3
  43.6 10.9 %collective-permute-done.2 = bf16[2,80,512]{2,1,0:T(8,128)(2,1)S(1)} collective-permute-done((bf16[2,80,512]{2,1,0:T(8,128)(2,1)S(1)}, bf16[2,80,512]{2,1,0:T(8,128)(2,1)S(1)}, u32[]{:S(2)}, u32[]{:S(2)}) %collective-permute-start.2) | collective-permute-done | bytes 163872 | tf_op jit(solution)/shard_map/ppermute | solution.py:166
  54.5 0.0 collective-permute-done.1
  54.5 0.1 pad_maximum_fusion.refs_0_
  54.6 2.3 %collective-permute-start.4 = (bf16[4,2,80,512]{3,2,1,0:T(8,128)(2,1)S(1)}, bf16[4,2,80,512]{3,2,1,0:T(8,128)(2,1)S(1)}, u32[]{:S(2)}, u32[]{:S(2)}) collective-permute-start(bf16[4,2,80,512]{3,2,1,0:T(8,128)(2,1)S(1)} %pad_maximum_fusion.refs_0_), channel_id=1, source_target_pairs={{0,8},{8,0},{1,9},{9,1},{2,10},{10,2},{3,11},{11,3},{4,12},{12,4},... | collective-permute-start | bytes 1966088 | tf_op jit(solution)/shard_map/ppermute | solution.py:168
  56.9 1.7 collective-permute-done.4.refs_1_
  58.6 7.0 %all-to-all-done = bf16[8,2,80,512]{3,2,1,0:T(8,128)(2,1)S(1)} async-done(((bf16[8,2,80,512]{3,2,1,0:T(8,128)(2,1)}), bf16[8,2,80,512]{3,2,1,0:T(8,128)(2,1)S(1)}, u32[]{:S(2)}, u32[]{:S(2)}) %all-to-all-start) | async-done | bytes 1310752 | tf_op jit(solution)/shard_map/all_to_all | solution.py:123
  65.6 1.7 shard_map.65
  67.4 17.9 %all_to_all.30 = bf16[4,4,2,32,512]{4,3,2,1,0:T(8,128)(2,1)S(1)} all-to-all(bf16[4,4,2,32,512]{4,3,2,1,0:T(8,128)(2,1)S(1)} %shard_map.65), channel_id=1, replica_groups=mesh['zh'=4,'zl'=4,'x'=4,'k'=2,'y'=8] {'x'}, dimensions={0} | all-to-all | bytes 2097152 | tf_op jit(solution)/shard_map/all_to_all | solution.py:123
  85.3 0.1 fusion
  85.5 34.1 %all_to_all.31 = bf16[4,2,32,512]{3,2,1,0:T(8,128)(2,1)S(1)} all-to-all(bf16[4,2,32,512]{3,2,1,0:T(8,128)(2,1)S(1)} %fusion), channel_id=1, replica_groups=mesh['zh'=4,'zl'=4,'x'=4,'k'=2,'y'=8] {'zh'}, dimensions={0} | all-to-all | bytes 524288 | tf_op jit(solution)/shard_map/all_to_all | solution.py:123
  119.6 0.1 fusion.1
  119.6 17.8 %all_to_all.32 = bf16[4,2,32,512]{3,2,1,0:T(8,128)(2,1)S(1)} all-to-all(bf16[4,2,32,512]{3,2,1,0:T(8,128)(2,1)S(1)} %broadcast_in_dim.17), channel_id=1, replica_groups=mesh['zh'=4,'zl'=4,'x'=4,'k'=2,'y'=8] {'zh'}, dimensions={0} | all-to-all | bytes 524288 | tf_op jit(solution)/shard_map/all_to_all | solution.py:123
  137.4 0.1 broadcast_in_dim.18
  137.5 12.6 %all_to_all.33.amp_ref = bf16[4,4,2,32,512]{4,3,2,1,0:T(8,128)(2,1)S(1)} all-to-all(bf16[4,4,2,32,512]{4,3,2,1,0:T(8,128)(2,1)S(1)} %broadcast_in_dim.18), channel_id=1, replica_groups=mesh['zh'=4,'zl'=4,'x'=4,'k'=2,'y'=8] {'x'}, dimensions={0} | all-to-all | bytes 2097152 | tf_op jit(solution)/shard_map/all_to_all | solution.py:123
  150.1 1.7 shard_map.66
  151.9 9.6 %collective-permute-start.5 = (bf16[4,2,80,512]{3,2,1,0:T(8,128)(2,1)S(1)}, bf16[4,2,80,512]{3,2,1,0:T(8,128)(2,1)S(1)}, u32[]{:S(2)}, u32[]{:S(2)}) collective-permute-start(bf16[4,2,80,512]{3,2,1,0:T(8,128)(2,1)S(1)} %get-tuple-element.22), channel_id=1, source_target_pairs={{0,8},{8,0},{1,9},{9,1},{2,10},{10,2},{3,11},{11,3},{4,12},{12,4},... | collective-permute-start | bytes 1966088 | tf_op jit(solution)/shard_map/ppermute | solution.py:175
  161.5 1.7 collective-permute-done.5
  163.2 0.2 add_convert_fusion
  163.3 24.9 %all_to_all.34 = bf16[4,2,80,512]{3,2,1,0:T(8,128)(2,1)S(1)} all-to-all(bf16[4,2,80,512]{3,2,1,0:T(8,128)(2,1)S(1)} %add_convert_fusion), channel_id=1, replica_groups=mesh['zh'=4,'zl'=4,'x'=4,'k'=2,'y'=8] {'zl'}, dimensions={0} | all-to-all | bytes 1310720 | tf_op jit(solution)/shard_map/all_to_all | solution.py:123
  188.2 0.1 add_bitcast_fusion
  188.3 1.0 copy.8
  (2 shorter events, 0.0 us)
Async XLA Ops:
  0.7 1.6 copy-start
  2.3 0.7 copy-start.1
  3.0 8.1 %copy-start.2 = (s32[2,2]{1,0:T(2,128)S(1)}, s32[2,2]{1,0:T(2,128)}, u32[]{:S(2)}) copy-start(s32[2,2]{1,0:T(2,128)} %pairs_ref.1) | copy-start | bytes 52
  3.0 8.2 %copy-start.3 = (f32[3]{0:T(128)S(1)}, f32[3]{0:T(128)}, u32[]{:S(2)}) copy-start(f32[3]{0:T(128)} %param.10) | copy-start | bytes 40
  6.5 11.0 %collective-permute-start = (bf16[2,80,512]{2,1,0:T(8,128)(2,1)S(1)}, bf16[2,80,512]{2,1,0:T(8,128)(2,1)S(1)}, u32[]{:S(2)}, u32[]{:S(2)}) collective-permute-start(bf16[2,80,512]{2,1,0:T(8,128)(2,1)S(1)} %get-tuple-element.14), channel_id=1, source_target_pairs={{0,0},{1,66},{2,132},{3,198},{4,9},{5,75},{6,141},{7,207},{8,1},{9... | collective-permute-start | bytes 491528 | tf_op jit(solution)/shard_map/ppermute | solution.py:150
  18.7 47.0 %all-to-all-start = ((bf16[8,2,80,512]{3,2,1,0:T(8,128)(2,1)}), bf16[8,2,80,512]{3,2,1,0:T(8,128)(2,1)S(1)}, u32[]{:S(2)}, u32[]{:S(2)}) async-start(bf16[8,2,80,512]{3,2,1,0:T(8,128)(2,1)} %broadcast_in_dim.16), calls=%async_computation | async-start | bytes 2621440 | tf_op jit(solution)/shard_map/all_to_all | solution.py:123
  30.8 12.7 %collective-permute-start.3 = (bf16[2,80,512]{2,1,0:T(8,128)(2,1)S(1)}, bf16[2,80,512]{2,1,0:T(8,128)(2,1)S(1)}, u32[]{:S(2)}, u32[]{:S(2)}) collective-permute-start(bf16[2,80,512]{2,1,0:T(8,128)(2,1)S(1)} %get-tuple-element.19), channel_id=1, source_target_pairs={{0,192},{64,0},{128,64},{192,128},{1,193},{65,1},{129,65},{193,129... | collective-permute-start | bytes 491528 | tf_op jit(solution)/shard_map/ppermute | solution.py:166
  39.4 15.0 %collective-permute-start.2 = (bf16[2,80,512]{2,1,0:T(8,128)(2,1)S(1)}, bf16[2,80,512]{2,1,0:T(8,128)(2,1)S(1)}, u32[]{:S(2)}, u32[]{:S(2)}) collective-permute-start(bf16[2,80,512]{2,1,0:T(8,128)(2,1)S(1)} %get-tuple-element.19), channel_id=1, source_target_pairs={{0,128},{64,192},{128,0},{192,64},{1,129},{65,193},{129,1},{193,65... | collective-permute-start | bytes 491528 | tf_op jit(solution)/shard_map/ppermute | solution.py:166
  41.4 13.1 %collective-permute-start.1 = (bf16[2,80,512]{2,1,0:T(8,128)(2,1)S(1)}, bf16[2,80,512]{2,1,0:T(8,128)(2,1)S(1)}, u32[]{:S(2)}, u32[]{:S(2)}) collective-permute-start(bf16[2,80,512]{2,1,0:T(8,128)(2,1)S(1)} %get-tuple-element.19), channel_id=1, source_target_pairs={{0,64},{64,128},{128,192},{192,0},{1,65},{65,129},{129,193},{193,1... | collective-permute-start | bytes 491528 | tf_op jit(solution)/shard_map/ppermute | solution.py:166
  54.6 4.0 %collective-permute-start.4 = (bf16[4,2,80,512]{3,2,1,0:T(8,128)(2,1)S(1)}, bf16[4,2,80,512]{3,2,1,0:T(8,128)(2,1)S(1)}, u32[]{:S(2)}, u32[]{:S(2)}) collective-permute-start(bf16[4,2,80,512]{3,2,1,0:T(8,128)(2,1)S(1)} %pad_maximum_fusion.refs_0_), channel_id=1, source_target_pairs={{0,8},{8,0},{1,9},{9,1},{2,10},{10,2},{3,11},{11,3},{4,12},{12,4},... | collective-permute-start | bytes 1966088 | tf_op jit(solution)/shard_map/ppermute | solution.py:168
  151.9 11.3 %collective-permute-start.5 = (bf16[4,2,80,512]{3,2,1,0:T(8,128)(2,1)S(1)}, bf16[4,2,80,512]{3,2,1,0:T(8,128)(2,1)S(1)}, u32[]{:S(2)}, u32[]{:S(2)}) collective-permute-start(bf16[4,2,80,512]{3,2,1,0:T(8,128)(2,1)S(1)} %get-tuple-element.22), channel_id=1, source_target_pairs={{0,8},{8,0},{1,9},{9,1},{2,10},{10,2},{3,11},{11,3},{4,12},{12,4},... | collective-permute-start | bytes 1966088 | tf_op jit(solution)/shard_map/ppermute | solution.py:175

commit v3 on v2

v3 whole, which is shorter than its diff:
```python
import jax
import jax.numpy as jnp
from jax import lax
from jax.experimental import pallas as pl
from jax.experimental.pallas import tpu as pltpu
from jax.sharding import Mesh, PartitionSpec as P

VMEM_LIMIT = 48 * 1024 * 1024
WIDE_LIMIT = 63 * 1024 * 1024
f32, bf16 = jnp.float32, jnp.bfloat16

NAMES = ("zh", "zl", "x", "k", "yh", "yl")
S1, S2 = "x", "zh"
GM = "zl"


def params():
    return pltpu.CompilerParams(vmem_limit_bytes=VMEM_LIMIT)


def transform(rows, coef, count, pairs, energies, place_of):
    occ, slots, basis = rows.shape
    width = coef.shape[1]
    step = 512
    steps = basis // step

    def kernel(
        count_hbm, pairs_hbm, energies_hbm, rows_hbm, coef_hbm,
        turn_a, turn_b, kept, given, energy,
        count_ref, pairs_ref, energies_ref, parts, coefs, held, sems, small,
    ):
        scalars = [
            pltpu.make_async_copy(count_hbm, count_ref, small.at[0]),
            pltpu.make_async_copy(pairs_hbm, pairs_ref, small.at[1]),
            pltpu.make_async_copy(energies_hbm, energies_ref, small.at[2]),
        ]
        copies = []
        for k in range(steps):
            span = pl.ds(k * step, step)
            copies.append(
                (
                    pltpu.make_async_copy(rows_hbm.at[:, :, span], parts.at[k], sems.at[0, k]),
                    pltpu.make_async_copy(coef_hbm.at[span], coefs.at[k], sems.at[1, k]),
                )
            )
        for pair in copies:
            for copy in pair:
                copy.start()
        for copy in scalars:
            copy.start()
        total = jnp.zeros((occ * slots, width), f32)
        for k in range(steps):
            for copy in copies[k]:
                copy.wait()
            part = parts[k].reshape(occ * slots, step)
            total += jnp.dot(part, coefs[k], preferred_element_type=f32)
        for copy in scalars:
            copy.wait()
        value = total.reshape(occ, slots, width)
        place = lax.broadcasted_iota(jnp.int32, (occ, slots, width), 1)
        held[...] = jnp.where(place < count_ref[0], value, 0.0).astype(bf16)
        half, core = place_of()
        turn_a[...] = held[pairs_ref[half, 0]]
        turn_b[...] = held[pairs_ref[1 - half, 0]]
        kept[...] = held[pairs_ref[core, 1]]
        given[...] = held[pairs_ref[1 - core, 1]]
        energy[0] = energies_ref[pairs_ref[core, 0]] + energies_ref[pairs_ref[core, 1]]

    out = jax.ShapeDtypeStruct((slots, width), bf16)
    hbm = pl.BlockSpec(memory_space=pl.ANY)
    vmem = pl.BlockSpec(memory_space=pltpu.VMEM)
    return pl.pallas_call(
        kernel,
        in_specs=[hbm] * 5,
        out_specs=[vmem] * 4 + [pl.BlockSpec(memory_space=pltpu.SMEM)],
        out_shape=[out] * 4 + [jax.ShapeDtypeStruct((1,), f32)],
        scratch_shapes=[
            pltpu.SMEM(count.shape, jnp.int32),
            pltpu.SMEM(pairs.shape, jnp.int32),
            pltpu.SMEM(energies.shape, f32),
            pltpu.VMEM((steps, occ, slots, step), bf16),
            pltpu.VMEM((steps, step, width), bf16),
            pltpu.VMEM((occ, slots, width), bf16),
            pltpu.SemaphoreType.DMA((2, steps)),
            pltpu.SemaphoreType.DMA((3,)),
        ],
        compiler_params=pltpu.CompilerParams(vmem_limit_bytes=WIDE_LIMIT),
    )(count, pairs, energies, rows, coef)


def flat(ref):
    return ref[...].reshape(-1, ref.shape[-1])


def coulomb_parts(side, first, second, n1, n2):
    groups, halves, slots, width = first[0].shape
    piece = width // (n1 * n2)

    def kernel(side_ref, near, low, high, *refs):
        out_ref = refs[-1]
        value = jnp.zeros((width, width), f32)
        held = [flat(near), jnp.concatenate([flat(low), flat(high)], axis=0)]
        for k in range(2):
            at = side_ref[0] if k == 0 else 1 - side_ref[0]
            b = jnp.concatenate([r[:, at].reshape(-1, width) for r in refs[:-1]], axis=0)
            value += lax.dot_general(
                held[k], b, (((0,), (0,)), ((), ())), preferred_element_type=f32
            )
        out_ref[...] = value.astype(bf16).reshape(n1, n2, 1, piece, width)

    return pl.pallas_call(
        kernel,
        grid=(halves,),
        in_specs=[pl.BlockSpec(memory_space=pltpu.SMEM)]
        + [pl.BlockSpec((f.shape[0], 1, slots, width), lambda h: (0, h, 0, 0)) for f in first]
        + [pl.BlockSpec(r.shape, lambda h: (0, 0, 0, 0)) for r in second],
        out_specs=pl.BlockSpec((n1, n2, 1, piece, width), lambda h: (0, 0, h, 0, 0)),
        out_shape=jax.ShapeDtypeStruct((n1, n2, halves, piece, width), bf16),
        compiler_params=params(),
    )(side, *first, *second)


def density_parts(side, targets, first, amplitude):
    groups, halves, slots, width = first[0].shape
    n1, n2, _, piece, _ = amplitude.shape

    def kernel(side_ref, targets_ref, near, low, high, amp_ref, out_ref):
        amps = [amp_ref[:, :, h].reshape(n1 * n2 * piece, width) for h in range(halves)]
        for k, refs in enumerate(((near,), (low, high))):
            value = 0.0
            for h in range(halves):
                a = jnp.concatenate([r[:, h].reshape(-1, width) for r in refs], axis=0)
                value += jnp.dot(a, amps[h], preferred_element_type=f32)
            value = value.astype(bf16).reshape(groups, slots, width)
            at = side_ref[0] if k == 0 else 1 - side_ref[0]
            for m in range(groups):
                out_ref[targets_ref[m], at] = value[m]

    smem = pl.BlockSpec(memory_space=pltpu.SMEM)
    vmem = pl.BlockSpec(memory_space=pltpu.VMEM)
    return pl.pallas_call(
        kernel,
        in_specs=[smem, smem] + [vmem] * 4,
        out_specs=vmem,
        out_shape=jax.ShapeDtypeStruct((groups, 2, slots, width), bf16),
        compiler_params=params(),
    )(side, targets, *first, amplitude)


def added(parts):
    total = parts[0].astype(f32)
    for k in range(1, parts.shape[0]):
        total = total + parts[k].astype(f32)
    return total


def exchange(parts, axis):
    return lax.all_to_all(parts, axis, 0, 0, tiled=True)


def spread(part, axis):
    copies = jnp.broadcast_to(part[None], (lax.axis_size(axis),) + part.shape)
    return exchange(lax.optimization_barrier(copies), axis)


def make_local(sizes):
    gm, cores, high, low = sizes[GM], sizes["k"], sizes["yh"], sizes["yl"]
    n1, n2 = sizes[S1], sizes[S2]
    cols = high * low
    order = (GM, "k", "yh", "yl")
    step = (0, 2, 1, 3)
    turns = [[], []]
    for m in range(gm):
        for k in range(cores):
            for y in range(cols):
                to_m, half = y % gm, y // gm
                to_y = step[to_m ^ m] * low + k
                for t in range(2):
                    to = (to_m * cores + (half ^ t)) * cols + to_y
                    turns[t].append(((m * cores + k) * cols + y, to))
    swap = [(0, 1), (1, 0)]
    up = [(y, (y + 1) % cols) for y in range(cols)]
    down = [(y, (y - 1) % cols) for y in range(cols)]
    across = [(m, m ^ 2) for m in range(gm)]
    beside = [(m, m ^ 1) for m in range(gm)]

    def column():
        return lax.axis_index("yh") * low + lax.axis_index("yl")

    def local(three_index, vir_coef, owner_count, pair_index, occ_energy, vir_energy):
        width = vir_coef.shape[1]
        core, group, side = lax.axis_index("k"), lax.axis_index(GM), lax.axis_index("yl")
        rows = jnp.transpose(three_index, (1, 0, 2))
        turn_a, turn_b, kept, given, energy = transform(
            rows, vir_coef, owner_count, pair_index, occ_energy,
            lambda: (column() // gm, lax.axis_index("k")),
        )
        turned = jnp.stack(
            [lax.ppermute(turn_a, order, turns[0]), lax.ppermute(turn_b, order, turns[1])]
        )

        piece = width // (n1 * n2)
        offset = lax.axis_index(S1) * (width // n1) + lax.axis_index(S2) * piece
        first_vir = jnp.stack(
            [
                lax.dynamic_slice_in_dim(vir_energy, (h * gm + group) * width + offset, piece)
                for h in (core, 1 - core)
            ]
        )
        second_vir = lax.dynamic_slice_in_dim(vir_energy, column() * width, width)
        denominator = energy[0] - first_vir[:, :, None] - second_vir
        targets = group ^ jnp.array(step, jnp.int32)
        flip = (side ^ core).astype(jnp.int32).reshape(1)
        second = jnp.stack([kept, lax.ppermute(given, "k", swap)])
        turned, second, denominator, targets, flip = lax.optimization_barrier(
            (turned, second, denominator, targets, flip)
        )

        near = spread(turned, "yh")
        second_held = jnp.stack([second, lax.ppermute(second, GM, across)])
        near, second_held = lax.optimization_barrier((near, second_held))
        second_beside = lax.ppermute(second_held, GM, beside)
        middle = high // 2
        far_low = lax.ppermute(near[:middle], ("yh", "yl"), up)
        far_high = lax.ppermute(near[middle:], ("yh", "yl"), down)
        first_all = [near, far_low, far_high]

        parts = coulomb_parts(flip, first_all, [second_held, second_beside], n1, n2)
        mine = added(exchange(parts, S1)).astype(bf16)
        share = added(exchange(mine, S2))
        amp = (share / denominator).astype(bf16)
        amp_all = spread(spread(amp, S2), S1)
        dens = added(exchange(density_parts(flip, targets, first_all, amp_all), GM))
        came = lax.ppermute(dens[1], "k", swap)
        out = [jnp.where(core == q, dens[0], came) for q in range(2)]
        return jnp.stack(out, axis=1)

    return local


def solution(mesh):
    aux, row, col = (mesh.shape[name] for name in ("aux", "row", "col"))
    sizes = {"zl": 4, "zh": aux // 4, "k": 2, "x": row // 2, "yh": col // 2, "yl": 2}
    fine = Mesh(mesh.devices.reshape([sizes[name] for name in NAMES]), NAMES)
    owners = ("zh", "zl", "x", "k")
    return jax.shard_map(
        make_local(sizes),
        mesh=fine,
        in_specs=(P(owners, None, None), P(None, ("yh", "yl")), P(owners), P(), P(), P()),
        out_specs=P(owners, None, ("yh", "yl")),
        check_vma=False,
    )
```

time: 190 us -> 180 us (0.947)
  blocking collectives: 107 us -> 100 us
  waiting for transfers between devices: 25.8 us -> 21.1 us
  local copies, waits for them, and re-layouts: 6.15 us -> 3.61 us
    ppermute x6 -> x8, starting transfers between devices: 29.2 us -> 38.7 us  [the longest x1 8.53 us: local(): lax.ppermute(turn_a, order, turns[0])]
    all_to_all x1, starting transfers between devices: 12.1 us -> 3.48 us  [exchange(): return lax.all_to_all(parts, axis, 0, 0, tiled=True)]
    all_to_all x5, blocking collectives: 107 us -> 100 us  [exchange(): return lax.all_to_all(parts, axis, 0, 0, tiled=True)]
    ppermute x6 -> x8, waiting for transfers between devices: 18.8 us -> 15.1 us  [the longest x1 5.03 us: local(): second_held = jnp.stack([second, lax.ppermute(second, GM, across)])]
    unnamed x8 -> x2, local copies, waits for them, and re-layouts: 2.3 us -> 0.01 us
  transfers between devices with their start and end apart: 7 -> 9, of which waited for: 5 -> 6; matrix products, arithmetic and copies ran while one was open for 1% -> 1% of each run, Pallas kernels for 0% -> 0%
where the time goes in v3:
time: 180 us; the launch traced here: 178 us
  blocking collectives  100 us (56%)
  starting transfers between devices  42.2 us (23%)
  waiting for transfers between devices  21.1 us (12%)
  Pallas kernels  7.35 us (4%)
  local copies, waits for them, and re-layouts  3.61 us (2%)
  other arithmetic  1.99 us (1%)
    all_to_all x5, blocking collectives, exchange(): return lax.all_to_all(parts, axis, 0, 0, tiled=True)  100 us
    ppermute x1, starting transfers between devices, local(): lax.ppermute(turn_a, order, turns[0])  8.53 us
    ppermute x1, starting transfers between devices, local(): second = jnp.stack([kept, lax.ppermute(given, 'k', swap)])  6.95 us
    ppermute x1, starting transfers between devices, local(): second_beside = lax.ppermute(second_held, GM, beside)  6.13 us
    all_to_all x1, waiting for transfers between devices, exchange(): return lax.all_to_all(parts, axis, 0, 0, tiled=True)  5.98 us
    ppermute x1, waiting for transfers between devices, local(): second_held = jnp.stack([second, lax.ppermute(second, GM, across)])  5.03 us
    ppermute x1, starting transfers between devices, local(): came = lax.ppermute(dens[1], 'k', swap)  4.7 us
    ppermute x1, starting transfers between devices, local(): far_high = lax.ppermute(near[middle:], ('yh', 'yl'), down)  4.57 us
  transfers between devices with their start and end apart: 9, of which 6 were waited for; matrix products, arithmetic and copies ran while one was open for 1% of the time, Pallas kernels for 0%

profile of v3, /device:TPU:1, one launch (start us, length us, event | category | flops | bytes accessed | tf_op | source)
XLA Modules:
  0.0 177.5 jit_solution(12701338699226069293)
XLA Ops:
  0.0 0.0 copy-start
  0.7 4.3 %shard_map.73 = (bf16[80,512]{1,0:T(8,128)(2,1)}, bf16[80,512]{1,0:T(8,128)(2,1)}, bf16[80,512]{1,0:T(8,128)(2,1)}, bf16[80,512]{1,0:T(8,128)(2,1)}, f32[1]{0:T(128)}) custom-call(s32[1]{0:T(128)S(6)} %copy.9.count_hbm, s32[2,2]{1,0:T(2,128)} %pairs_hbm.1, f32[3]{0:T(128)} %energies_hbm.1, bf16[3,80,4608]{2,1,0:T(8,128)(2,1)} %bitcast.31, ...), custom_call_target="tpu_custom_call" | custom-call | tf_op jit(solution)/shard_map/pallas_call | solution.py:72
  5.0 4.0 %collective-permute-start.1 = (bf16[80,512]{1,0:T(8,128)(2,1)}, bf16[80,512]{1,0:T(8,128)(2,1)S(1)}, u32[]{:S(2)}, u32[]{:S(2)}) collective-permute-start(bf16[80,512]{1,0:T(8,128)(2,1)} %get-tuple-element.18), channel_id=1, source_target_pairs={{0,8},{1,76},{2,138},{3,206},{4,0},{5,68},{6,130},{7,198},{8,9},{9... | collective-permute-start | bytes 245768 | tf_op jit(solution)/shard_map/ppermute | solution.py:199
  9.0 8.5 %collective-permute-start = (bf16[80,512]{1,0:T(8,128)(2,1)}, bf16[80,512]{1,0:T(8,128)(2,1)S(1)}, u32[]{:S(2)}, u32[]{:S(2)}) collective-permute-start(bf16[80,512]{1,0:T(8,128)(2,1)} %get-tuple-element.17), channel_id=1, source_target_pairs={{0,0},{1,68},{2,130},{3,198},{4,8},{5,76},{6,138},{7,206},{8,1},{9... | collective-permute-start | bytes 245768 | tf_op jit(solution)/shard_map/ppermute | solution.py:199
  17.6 6.9 %collective-permute-start.2 = (bf16[80,512]{1,0:T(8,128)(2,1)}, bf16[80,512]{1,0:T(8,128)(2,1)S(1)}, u32[]{:S(2)}, u32[]{:S(2)}) collective-permute-start(bf16[80,512]{1,0:T(8,128)(2,1)} %get-tuple-element.20), channel_id=1, source_target_pairs={{0,8},{8,0},{1,9},{9,1},{2,10},{10,2},{3,11},{11,3},{4,12},{12,4},... | collective-permute-start | bytes 245768 | tf_op jit(solution)/shard_map/ppermute | solution.py:214
  24.5 0.8 dynamic_slice.11
  25.3 0.8 dynamic-slice_bitcast_fusion.1
  26.1 0.6 maximum_subtract_fusion
  26.7 0.1 broadcast_subtract_fusion
  26.8 0.0 copy-done
  26.8 0.0 collective-permute-done.1
  26.8 4.0 %collective-permute-done = bf16[80,512]{1,0:T(8,128)(2,1)S(1)} collective-permute-done((bf16[80,512]{1,0:T(8,128)(2,1)}, bf16[80,512]{1,0:T(8,128)(2,1)S(1)}, u32[]{:S(2)}, u32[]{:S(2)}) %collective-permute-start) | collective-permute-done | bytes 81952 | tf_op jit(solution)/shard_map/ppermute | solution.py:199
  30.8 0.0 collective-permute-done.2
  30.9 0.9 pad_maximum_fusion.3
  31.8 0.9 broadcast_in_dim.6
  32.7 3.5 %all-to-all-start = ((bf16[4,2,80,512]{3,2,1,0:T(8,128)(2,1)}), bf16[4,2,80,512]{3,2,1,0:T(8,128)(2,1)S(1)}, u32[]{:S(2)}, u32[]{:S(2)}) async-start(bf16[4,2,80,512]{3,2,1,0:T(8,128)(2,1)} %broadcast_in_dim.6), calls=%async_computation | async-start | bytes 1310720 | tf_op jit(solution)/shard_map/all_to_all | solution.py:158
  36.2 1.9 %collective-permute-start.3 = (bf16[2,80,512]{2,1,0:T(8,128)(2,1)S(1)}, bf16[2,80,512]{2,1,0:T(8,128)(2,1)S(1)}, u32[]{:S(2)}, u32[]{:S(2)}) collective-permute-start(bf16[2,80,512]{2,1,0:T(8,128)(2,1)S(1)} %pad_maximum_fusion.3), channel_id=1, source_target_pairs={{0,128},{64,192},{128,0},{192,64},{1,129},{65,193},{129,1},{193,65... | collective-permute-start | bytes 491528 | tf_op jit(solution)/shard_map/ppermute | solution.py:220
  38.1 5.0 %collective-permute-done.3 = bf16[2,80,512]{2,1,0:T(8,128)(2,1)S(1)} collective-permute-done((bf16[2,80,512]{2,1,0:T(8,128)(2,1)S(1)}, bf16[2,80,512]{2,1,0:T(8,128)(2,1)S(1)}, u32[]{:S(2)}, u32[]{:S(2)}) %collective-permute-start.3) | collective-permute-done | bytes 163872 | tf_op jit(solution)/shard_map/ppermute | solution.py:220
  43.1 6.0 %all-to-all-done.near = bf16[4,2,80,512]{3,2,1,0:T(8,128)(2,1)S(1)} async-done(((bf16[4,2,80,512]{3,2,1,0:T(8,128)(2,1)}), bf16[4,2,80,512]{3,2,1,0:T(8,128)(2,1)S(1)}, u32[]{:S(2)}, u32[]{:S(2)}) %all-to-all-start) | async-done | bytes 655392 | tf_op jit(solution)/shard_map/all_to_all | solution.py:158
  49.2 1.9 %collective-permute-start.4 = (bf16[2,2,80,512]{3,2,1,0:T(8,128)(2,1)S(1)}, bf16[2,2,80,512]{3,2,1,0:T(8,128)(2,1)S(1)}, u32[]{:S(2)}, u32[]{:S(2)}) collective-permute-start(bf16[2,2,80,512]{3,2,1,0:T(8,128)(2,1)S(1)} %get-tuple-element.30), channel_id=1, source_target_pairs={{0,1},{1,2},{2,3},{3,4},{4,5},{5,6},{6,7},{7,0},{8,9},{9,10},{10,1... | collective-permute-start | bytes 983048 | tf_op jit(solution)/shard_map/ppermute | solution.py:224
  51.1 4.6 %collective-permute-start.5 = (bf16[2,2,80,512]{3,2,1,0:T(8,128)(2,1)S(1)}, bf16[2,2,80,512]{3,2,1,0:T(8,128)(2,1)S(1)}, u32[]{:S(2)}, u32[]{:S(2)}) collective-permute-start(bf16[2,2,80,512]{3,2,1,0:T(8,128)(2,1)S(1)} %get-tuple-element.29), channel_id=1, source_target_pairs={{0,7},{1,0},{2,1},{3,2},{4,3},{5,4},{6,5},{7,6},{8,15},{9,8},{10,9... | collective-permute-start | bytes 983048 | tf_op jit(solution)/shard_map/ppermute | solution.py:225
  55.7 6.1 %collective-permute-start.6 = (bf16[2,2,80,512]{3,2,1,0:T(8,128)(2,1)S(1)}, bf16[2,2,80,512]{3,2,1,0:T(8,128)(2,1)S(1)}, u32[]{:S(2)}, u32[]{:S(2)}) collective-permute-start(bf16[2,2,80,512]{3,2,1,0:T(8,128)(2,1)S(1)} %pad_maximum_fusion.refs_0_), channel_id=1, source_target_pairs={{0,64},{64,0},{128,192},{192,128},{1,65},{65,1},{129,193},{193,129... | collective-permute-start | bytes 983048 | tf_op jit(solution)/shard_map/ppermute | solution.py:222
  61.8 0.0 collective-permute-done.4.low
  61.8 0.9 collective-permute-done.5.high
  62.7 4.2 %collective-permute-done.6.refs_1_ = bf16[2,2,80,512]{3,2,1,0:T(8,128)(2,1)S(1)} collective-permute-done((bf16[2,2,80,512]{3,2,1,0:T(8,128)(2,1)S(1)}, bf16[2,2,80,512]{3,2,1,0:T(8,128)(2,1)S(1)}, u32[]{:S(2)}, u32[]{:S(2)}) %collective-permute-start.6) | collective-permute-done | bytes 327712 | tf_op jit(solution)/shard_map/ppermute | solution.py:222
  66.9 1.7 shard_map.74
  68.6 14.9 %all_to_all.30 = bf16[4,4,2,32,512]{4,3,2,1,0:T(8,128)(2,1)S(1)} all-to-all(bf16[4,4,2,32,512]{4,3,2,1,0:T(8,128)(2,1)S(1)} %shard_map.74), channel_id=1, replica_groups=mesh['zh'=4,'zl'=4,'x'=4,'k'=2,'yh'=4,'yl'=2] {'x'}, dimensions={0} | all-to-all | bytes 2097152 | tf_op jit(solution)/shard_map/all_to_all | solution.py:158
  83.5 0.1 fusion
  83.6 25.7 %all_to_all.31 = bf16[4,2,32,512]{3,2,1,0:T(8,128)(2,1)S(1)} all-to-all(bf16[4,2,32,512]{3,2,1,0:T(8,128)(2,1)S(1)} %fusion), channel_id=1, replica_groups=mesh['zh'=4,'zl'=4,'x'=4,'k'=2,'yh'=4,'yl'=2] {'zh'}, dimensions={0} | all-to-all | bytes 524288 | tf_op jit(solution)/shard_map/all_to_all | solution.py:158
  109.4 15.6 %all_to_all.32 = bf16[4,2,32,512]{3,2,1,0:T(8,128)(2,1)S(1)} all-to-all(bf16[4,2,32,512]{3,2,1,0:T(8,128)(2,1)S(1)} %broadcast_in_dim.7), channel_id=1, replica_groups=mesh['zh'=4,'zl'=4,'x'=4,'k'=2,'yh'=4,'yl'=2] {'zh'}, dimensions={0} | all-to-all | bytes 524288 | tf_op jit(solution)/shard_map/all_to_all | solution.py:158
  125.0 0.1 broadcast_in_dim.8
  125.1 12.2 %all_to_all.33.amp_ref = bf16[4,4,2,32,512]{4,3,2,1,0:T(8,128)(2,1)S(1)} all-to-all(bf16[4,4,2,32,512]{4,3,2,1,0:T(8,128)(2,1)S(1)} %broadcast_in_dim.8), channel_id=1, replica_groups=mesh['zh'=4,'zl'=4,'x'=4,'k'=2,'yh'=4,'yl'=2] {'x'}, dimensions={0} | all-to-all | bytes 2097152 | tf_op jit(solution)/shard_map/all_to_all | solution.py:158
  137.3 1.4 shard_map.75
  138.6 32.0 %all_to_all.34 = bf16[4,2,80,512]{3,2,1,0:T(8,128)(2,1)S(1)} all-to-all(bf16[4,2,80,512]{3,2,1,0:T(8,128)(2,1)S(1)} %shard_map.75), channel_id=1, replica_groups=mesh['zh'=4,'zl'=4,'x'=4,'k'=2,'yh'=4,'yl'=2] {'zl'}, dimensions={0} | all-to-all | bytes 1310720 | tf_op jit(solution)/shard_map/all_to_all | solution.py:158
  170.7 0.1 convert_add_fusion
  170.8 4.7 %collective-permute-start.7 = (f32[80,512]{1,0:T(8,128)S(1)}, f32[80,512]{1,0:T(8,128)S(1)}, u32[]{:S(2)}, u32[]{:S(2)}) collective-permute-start(f32[80,512]{1,0:T(8,128)S(1)} %slice_bitcast_fusion), channel_id=1, source_target_pairs={{0,8},{8,0},{1,9},{9,1},{2,10},{10,2},{3,11},{11,3},{4,12},{12,4},... | collective-permute-start | bytes 491528 | tf_op jit(solution)/shard_map/ppermute | solution.py:234
  175.5 1.0 collective-permute-done.7
  176.5 1.0 copy.8
  (9 shorter events, 0.2 us)
Async XLA Ops:
  0.0 26.8 %copy-start = (s32[4]{0:T(128)S(1)}, s32[4]{0:T(128)}, u32[]{:S(2)}) copy-start(s32[4]{0:T(128)} %constant.41.clone) | copy-start | bytes 52
  5.0 21.9 %collective-permute-start.1 = (bf16[80,512]{1,0:T(8,128)(2,1)}, bf16[80,512]{1,0:T(8,128)(2,1)S(1)}, u32[]{:S(2)}, u32[]{:S(2)}) collective-permute-start(bf16[80,512]{1,0:T(8,128)(2,1)} %get-tuple-element.18), channel_id=1, source_target_pairs={{0,8},{1,76},{2,138},{3,206},{4,0},{5,68},{6,130},{7,198},{8,9},{9... | collective-permute-start | bytes 245768 | tf_op jit(solution)/shard_map/ppermute | solution.py:199
  9.0 21.8 %collective-permute-start = (bf16[80,512]{1,0:T(8,128)(2,1)}, bf16[80,512]{1,0:T(8,128)(2,1)S(1)}, u32[]{:S(2)}, u32[]{:S(2)}) collective-permute-start(bf16[80,512]{1,0:T(8,128)(2,1)} %get-tuple-element.17), channel_id=1, source_target_pairs={{0,0},{1,68},{2,130},{3,198},{4,8},{5,76},{6,138},{7,206},{8,1},{9... | collective-permute-start | bytes 245768 | tf_op jit(solution)/shard_map/ppermute | solution.py:199
  17.6 13.3 %collective-permute-start.2 = (bf16[80,512]{1,0:T(8,128)(2,1)}, bf16[80,512]{1,0:T(8,128)(2,1)S(1)}, u32[]{:S(2)}, u32[]{:S(2)}) collective-permute-start(bf16[80,512]{1,0:T(8,128)(2,1)} %get-tuple-element.20), channel_id=1, source_target_pairs={{0,8},{8,0},{1,9},{9,1},{2,10},{10,2},{3,11},{11,3},{4,12},{12,4},... | collective-permute-start | bytes 245768 | tf_op jit(solution)/shard_map/ppermute | solution.py:214
  32.7 16.5 %all-to-all-start = ((bf16[4,2,80,512]{3,2,1,0:T(8,128)(2,1)}), bf16[4,2,80,512]{3,2,1,0:T(8,128)(2,1)S(1)}, u32[]{:S(2)}, u32[]{:S(2)}) async-start(bf16[4,2,80,512]{3,2,1,0:T(8,128)(2,1)} %broadcast_in_dim.6), calls=%async_computation | async-start | bytes 1310720 | tf_op jit(solution)/shard_map/all_to_all | solution.py:158
  36.2 7.0 %collective-permute-start.3 = (bf16[2,80,512]{2,1,0:T(8,128)(2,1)S(1)}, bf16[2,80,512]{2,1,0:T(8,128)(2,1)S(1)}, u32[]{:S(2)}, u32[]{:S(2)}) collective-permute-start(bf16[2,80,512]{2,1,0:T(8,128)(2,1)S(1)} %pad_maximum_fusion.3), channel_id=1, source_target_pairs={{0,128},{64,192},{128,0},{192,64},{1,129},{65,193},{129,1},{193,65... | collective-permute-start | bytes 491528 | tf_op jit(solution)/shard_map/ppermute | solution.py:220
  49.2 12.6 %collective-permute-start.4 = (bf16[2,2,80,512]{3,2,1,0:T(8,128)(2,1)S(1)}, bf16[2,2,80,512]{3,2,1,0:T(8,128)(2,1)S(1)}, u32[]{:S(2)}, u32[]{:S(2)}) collective-permute-start(bf16[2,2,80,512]{3,2,1,0:T(8,128)(2,1)S(1)} %get-tuple-element.30), channel_id=1, source_target_pairs={{0,1},{1,2},{2,3},{3,4},{4,5},{5,6},{6,7},{7,0},{8,9},{9,10},{10,1... | collective-permute-start | bytes 983048 | tf_op jit(solution)/shard_map/ppermute | solution.py:224
  51.1 11.6 %collective-permute-start.5 = (bf16[2,2,80,512]{3,2,1,0:T(8,128)(2,1)S(1)}, bf16[2,2,80,512]{3,2,1,0:T(8,128)(2,1)S(1)}, u32[]{:S(2)}, u32[]{:S(2)}) collective-permute-start(bf16[2,2,80,512]{3,2,1,0:T(8,128)(2,1)S(1)} %get-tuple-element.29), channel_id=1, source_target_pairs={{0,7},{1,0},{2,1},{3,2},{4,3},{5,4},{6,5},{7,6},{8,15},{9,8},{10,9... | collective-permute-start | bytes 983048 | tf_op jit(solution)/shard_map/ppermute | solution.py:225
  55.7 11.2 %collective-permute-start.6 = (bf16[2,2,80,512]{3,2,1,0:T(8,128)(2,1)S(1)}, bf16[2,2,80,512]{3,2,1,0:T(8,128)(2,1)S(1)}, u32[]{:S(2)}, u32[]{:S(2)}) collective-permute-start(bf16[2,2,80,512]{3,2,1,0:T(8,128)(2,1)S(1)} %pad_maximum_fusion.refs_0_), channel_id=1, source_target_pairs={{0,64},{64,0},{128,192},{192,128},{1,65},{65,1},{129,193},{193,129... | collective-permute-start | bytes 983048 | tf_op jit(solution)/shard_map/ppermute | solution.py:222
  170.8 5.7 %collective-permute-start.7 = (f32[80,512]{1,0:T(8,128)S(1)}, f32[80,512]{1,0:T(8,128)S(1)}, u32[]{:S(2)}, u32[]{:S(2)}) collective-permute-start(f32[80,512]{1,0:T(8,128)S(1)} %slice_bitcast_fusion), channel_id=1, source_target_pairs={{0,8},{8,0},{1,9},{9,1},{2,10},{10,2},{3,11},{11,3},{4,12},{12,4},... | collective-permute-start | bytes 491528 | tf_op jit(solution)/shard_map/ppermute | solution.py:234

commit v4 on v3

--- a/solution.py
+++ b/solution.py
@@ -102,7 +102,7 @@
         held = [flat(near), jnp.concatenate([flat(low), flat(high)], axis=0)]
         for k in range(2):
             at = side_ref[0] if k == 0 else 1 - side_ref[0]
-            b = jnp.concatenate([r[:, at].reshape(-1, width) for r in refs[:-1]], axis=0)
+            b = jnp.concatenate([r[at] for r in refs[:-1]], axis=0)
             value += lax.dot_general(
                 held[k], b, (((0,), (0,)), ((), ())), preferred_element_type=f32
             )
@@ -113,7 +113,7 @@
         grid=(halves,),
         in_specs=[pl.BlockSpec(memory_space=pltpu.SMEM)]
         + [pl.BlockSpec((f.shape[0], 1, slots, width), lambda h: (0, h, 0, 0)) for f in first]
-        + [pl.BlockSpec(r.shape, lambda h: (0, 0, 0, 0)) for r in second],
+        + [pl.BlockSpec(r.shape, lambda h: (0, 0, 0)) for r in second],
         out_specs=pl.BlockSpec((n1, n2, 1, piece, width), lambda h: (0, 0, h, 0, 0)),
         out_shape=jax.ShapeDtypeStruct((n1, n2, halves, piece, width), bf16),
         compiler_params=params(),
@@ -154,8 +154,52 @@
     return total
 
 
+def finish(core, parts, came):
+    groups, members, slots, width = parts.shape
+
+    def kernel(core_ref, parts_ref, came_ref, out_ref):
+        total = parts_ref[0, 0].astype(f32)
+        for m in range(1, groups):
+            total += parts_ref[m, 0].astype(f32)
+        came = came_ref[...]
+        own = core_ref[0] == 0
+        out_ref[:, 0, :] = jnp.where(own, total, came)
+        out_ref[:, 1, :] = jnp.where(own, came, total)
+
+    vmem = pl.BlockSpec(memory_space=pltpu.VMEM)
+    return pl.pallas_call(
+        kernel,
+        grid=(1,),
+        in_specs=[
+            pl.BlockSpec(memory_space=pltpu.SMEM),
+            pl.BlockSpec((groups, 1, slots, width), lambda i: (0, 0, 0, 0)),
+            pl.BlockSpec((slots, width), lambda i: (0, 0)),
+        ],
+        out_specs=pl.BlockSpec((slots, 2, width), lambda i: (0, 0, 0)),
+        out_shape=jax.ShapeDtypeStruct((slots, 2, width), f32),
+        compiler_params=params(),
+    )(core.astype(jnp.int32).reshape(1), parts, came)
+
+
 def exchange(parts, axis):
     return lax.all_to_all(parts, axis, 0, 0, tiled=True)
+
+
+def copied(parts, count):
+    def kernel(*refs):
+        for n in range(count):
+            for i, part in enumerate(refs[:-1]):
+                refs[-1][n, i] = part[...]
+
+    vmem = pl.BlockSpec(memory_space=pltpu.VMEM)
+    shape = (count, len(parts)) + parts[0].shape
+    return pl.pallas_call(
+        kernel,
+        in_specs=[vmem] * len(parts),
+        out_specs=vmem,
+        out_shape=jax.ShapeDtypeStruct(shape, parts[0].dtype),
+        compiler_params=params(),
+    )(*parts)
 
 
 def spread(part, axis):
@@ -168,21 +212,18 @@
     n1, n2 = sizes[S1], sizes[S2]
     cols = high * low
     order = (GM, "k", "yh", "yl")
-    step = (0, 2, 1, 3)
     turns = [[], []]
     for m in range(gm):
         for k in range(cores):
             for y in range(cols):
                 to_m, half = y % gm, y // gm
-                to_y = step[to_m ^ m] * low + k
+                to_y = (to_m ^ m) * low + k
                 for t in range(2):
                     to = (to_m * cores + (half ^ t)) * cols + to_y
                     turns[t].append(((m * cores + k) * cols + y, to))
     swap = [(0, 1), (1, 0)]
     up = [(y, (y + 1) % cols) for y in range(cols)]
     down = [(y, (y - 1) % cols) for y in range(cols)]
-    across = [(m, m ^ 2) for m in range(gm)]
-    beside = [(m, m ^ 1) for m in range(gm)]
 
     def column():
         return lax.axis_index("yh") * low + lax.axis_index("yl")
@@ -195,9 +236,7 @@
             rows, vir_coef, owner_count, pair_index, occ_energy,
             lambda: (column() // gm, lax.axis_index("k")),
         )
-        turned = jnp.stack(
-            [lax.ppermute(turn_a, order, turns[0]), lax.ppermute(turn_b, order, turns[1])]
-        )
+        turned = [lax.ppermute(turn_a, order, turns[0]), lax.ppermute(turn_b, order, turns[1])]
 
         piece = width // (n1 * n2)
         offset = lax.axis_index(S1) * (width // n1) + lax.axis_index(S2) * piece
@@ -209,31 +248,30 @@
         )
         second_vir = lax.dynamic_slice_in_dim(vir_energy, column() * width, width)
         denominator = energy[0] - first_vir[:, :, None] - second_vir
-        targets = group ^ jnp.array(step, jnp.int32)
+        targets = group ^ jnp.arange(gm, dtype=jnp.int32)
         flip = (side ^ core).astype(jnp.int32).reshape(1)
         second = jnp.stack([kept, lax.ppermute(given, "k", swap)])
         turned, second, denominator, targets, flip = lax.optimization_barrier(
             (turned, second, denominator, targets, flip)
         )
 
-        near = spread(turned, "yh")
-        second_held = jnp.stack([second, lax.ppermute(second, GM, across)])
-        near, second_held = lax.optimization_barrier((near, second_held))
-        second_beside = lax.ppermute(second_held, GM, beside)
+        near = exchange(copied(turned, high), "yh")
+        others = [lax.ppermute(second, GM, [(m, m ^ d) for m in range(gm)]) for d in (2, 1, 3)]
+        near, others = lax.optimization_barrier((near, others))
+        second_all = [second, others[1], others[0], others[2]]
         middle = high // 2
         far_low = lax.ppermute(near[:middle], ("yh", "yl"), up)
         far_high = lax.ppermute(near[middle:], ("yh", "yl"), down)
         first_all = [near, far_low, far_high]
 
-        parts = coulomb_parts(flip, first_all, [second_held, second_beside], n1, n2)
+        parts = coulomb_parts(flip, first_all, second_all, n1, n2)
         mine = added(exchange(parts, S1)).astype(bf16)
         share = added(exchange(mine, S2))
         amp = (share / denominator).astype(bf16)
         amp_all = spread(spread(amp, S2), S1)
-        dens = added(exchange(density_parts(flip, targets, first_all, amp_all), GM))
-        came = lax.ppermute(dens[1], "k", swap)
-        out = [jnp.where(core == q, dens[0], came) for q in range(2)]
-        return jnp.stack(out, axis=1)
+        dens = exchange(density_parts(flip, targets, first_all, amp_all), GM)
+        given = added(dens[:, 1])
+        return finish(core, dens, lax.ppermute(given, "k", swap))
 
     return local
 

time: 180 us -> 177 us (0.983)
  the two profiles are of different devices: /device:TPU:1 before, /device:TPU:17 now
where the time goes in v4:
time: 177 us; the launch traced here: 176 us
  blocking collectives  104 us (59%)
  starting transfers between devices  41.7 us (24%)
  waiting for transfers between devices  16.7 us (9%)
  Pallas kernels  9.07 us (5%)
  other arithmetic  1.92 us (1%)
    all_to_all x5, blocking collectives, exchange(): return lax.all_to_all(parts, axis, 0, 0, tiled=True)  104 us
    ppermute x1, starting transfers between devices, local(): lax.ppermute(turn_a, order, turns[0])  9.72 us
    ppermute x3, starting transfers between devices, local(): lax.ppermute(second, GM, [(m, m ^ d) for m in range(gm)])  9.26 us
    all_to_all x1, starting transfers between devices, exchange(): return lax.all_to_all(parts, axis, 0, 0, tiled=True)  8.65 us
    ppermute x3, waiting for transfers between devices, local(): lax.ppermute(second, GM, [(m, m ^ d) for m in range(gm)])  6.81 us
    ppermute x1, starting transfers between devices, local(): return finish(core, dens, lax.ppermute(given, 'k', swap))  4.68 us
    pallas_call x1, Pallas kernels, transform(): pl.pallas_call(kernel, in_specs=[hbm] * 5, out_specs=[vmem] * 4 + [pl.Blo...  4.31 us
    ppermute x1, waiting for transfers between devices, local(): far_high = lax.ppermute(near[middle:], ('yh', 'yl'), down)  3.76 us
  transfers between devices with their start and end apart: 10, of which 5 were waited for; matrix products, arithmetic and copies ran while one was open for 2% of the time, Pallas kernels for 0%

profile of v4, /device:TPU:17, one launch (start us, length us, event | category | flops | bytes accessed | tf_op | source)
XLA Modules:
  0.0 176.3 jit_solution(7129119693379963809)
XLA Ops:
  0.7 4.3 %shard_map.64 = (bf16[80,512]{1,0:T(8,128)(2,1)}, bf16[80,512]{1,0:T(8,128)(2,1)}, bf16[80,512]{1,0:T(8,128)(2,1)}, bf16[80,512]{1,0:T(8,128)(2,1)}, f32[1]{0:T(128)}) custom-call(s32[1]{0:T(128)S(6)} %copy.7.count_hbm, s32[2,2]{1,0:T(2,128)} %pairs_hbm.1, f32[3]{0:T(128)} %energies_hbm.1, bf16[3,80,4608]{2,1,0:T(8,128)(2,1)} %bitcast.18, ...), custom_call_target="tpu_custom_call" | custom-call | tf_op jit(solution)/shard_map/pallas_call | solution.py:72
  5.0 9.7 %collective-permute-start = (bf16[80,512]{1,0:T(8,128)(2,1)}, bf16[80,512]{1,0:T(8,128)(2,1)S(1)}, u32[]{:S(2)}, u32[]{:S(2)}) collective-permute-start(bf16[80,512]{1,0:T(8,128)(2,1)} %get-tuple-element.20), channel_id=1, source_target_pairs={{0,0},{1,66},{2,132},{3,198},{4,8},{5,74},{6,140},{7,206},{8,1},{9... | collective-permute-start | bytes 245768 | tf_op jit(solution)/shard_map/ppermute | solution.py:239
  14.7 1.9 %collective-permute-start.1 = (bf16[80,512]{1,0:T(8,128)(2,1)}, bf16[80,512]{1,0:T(8,128)(2,1)S(1)}, u32[]{:S(2)}, u32[]{:S(2)}) collective-permute-start(bf16[80,512]{1,0:T(8,128)(2,1)} %get-tuple-element.21), channel_id=1, source_target_pairs={{0,8},{1,74},{2,140},{3,206},{4,0},{5,66},{6,132},{7,198},{8,9},{9... | collective-permute-start | bytes 245768 | tf_op jit(solution)/shard_map/ppermute | solution.py:239
  16.6 2.2 %collective-permute-start.2 = (bf16[80,512]{1,0:T(8,128)(2,1)}, bf16[80,512]{1,0:T(8,128)(2,1)S(1)}, u32[]{:S(2)}, u32[]{:S(2)}) collective-permute-start(bf16[80,512]{1,0:T(8,128)(2,1)} %get-tuple-element.23), channel_id=1, source_target_pairs={{0,8},{8,0},{1,9},{9,1},{2,10},{10,2},{3,11},{11,3},{4,12},{12,4},... | collective-permute-start | bytes 245768 | tf_op jit(solution)/shard_map/ppermute | solution.py:253
  18.8 0.8 dynamic_slice.11
  19.6 0.8 dynamic-slice_bitcast_fusion.1
  20.4 0.7 maximum_subtract_fusion
  21.1 0.1 broadcast_subtract_fusion
  21.2 0.0 collective-permute-done.2
  21.2 0.9 pad_maximum_fusion.refs_0_
  22.1 0.0 collective-permute-done.refs_0_
  22.1 3.2 %collective-permute-done.1.refs_1_ = bf16[80,512]{1,0:T(8,128)(2,1)S(1)} collective-permute-done((bf16[80,512]{1,0:T(8,128)(2,1)}, bf16[80,512]{1,0:T(8,128)(2,1)S(1)}, u32[]{:S(2)}, u32[]{:S(2)}) %collective-permute-start.1) | collective-permute-done | bytes 81952 | tf_op jit(solution)/shard_map/ppermute | solution.py:239
  25.3 0.9 shard_map.65
  26.2 8.7 %all-to-all-start = ((bf16[4,2,80,512]{3,2,1,0:T(8,128)(2,1)}), bf16[4,2,80,512]{3,2,1,0:T(8,128)(2,1)S(1)}, u32[]{:S(2)}, u32[]{:S(2)}) async-start(bf16[4,2,80,512]{3,2,1,0:T(8,128)(2,1)} %shard_map.65), calls=%async_computation | async-start | bytes 1310720 | tf_op jit(solution)/shard_map/all_to_all | solution.py:185
  34.8 1.9 %collective-permute-start.5 = (bf16[2,80,512]{2,1,0:T(8,128)(2,1)S(1)}, bf16[2,80,512]{2,1,0:T(8,128)(2,1)S(1)}, u32[]{:S(2)}, u32[]{:S(2)}) collective-permute-start(bf16[2,80,512]{2,1,0:T(8,128)(2,1)S(1)} %pad_maximum_fusion.refs_0_), channel_id=1, source_target_pairs={{0,192},{64,128},{128,64},{192,0},{1,193},{65,129},{129,65},{193,1... | collective-permute-start | bytes 491528 | tf_op jit(solution)/shard_map/ppermute | solution.py:259
  36.8 1.9 %collective-permute-start.4 = (bf16[2,80,512]{2,1,0:T(8,128)(2,1)S(1)}, bf16[2,80,512]{2,1,0:T(8,128)(2,1)S(1)}, u32[]{:S(2)}, u32[]{:S(2)}) collective-permute-start(bf16[2,80,512]{2,1,0:T(8,128)(2,1)S(1)} %pad_maximum_fusion.refs_0_), channel_id=1, source_target_pairs={{0,64},{64,0},{128,192},{192,128},{1,65},{65,1},{129,193},{193,129... | collective-permute-start | bytes 491528 | tf_op jit(solution)/shard_map/ppermute | solution.py:259
  38.7 5.4 %collective-permute-start.3 = (bf16[2,80,512]{2,1,0:T(8,128)(2,1)S(1)}, bf16[2,80,512]{2,1,0:T(8,128)(2,1)S(1)}, u32[]{:S(2)}, u32[]{:S(2)}) collective-permute-start(bf16[2,80,512]{2,1,0:T(8,128)(2,1)S(1)} %pad_maximum_fusion.refs_0_), channel_id=1, source_target_pairs={{0,128},{64,192},{128,0},{192,64},{1,129},{65,193},{129,1},{193,65... | collective-permute-start | bytes 491528 | tf_op jit(solution)/shard_map/ppermute | solution.py:259
  44.1 0.0 collective-permute-done.5.refs_3_
  44.1 6.8 %collective-permute-done.4.refs_1_ = bf16[2,80,512]{2,1,0:T(8,128)(2,1)S(1)} collective-permute-done((bf16[2,80,512]{2,1,0:T(8,128)(2,1)S(1)}, bf16[2,80,512]{2,1,0:T(8,128)(2,1)S(1)}, u32[]{:S(2)}, u32[]{:S(2)}) %collective-permute-start.4) | collective-permute-done | bytes 163872 | tf_op jit(solution)/shard_map/ppermute | solution.py:259
  50.9 0.0 collective-permute-done.3.refs_2_
  50.9 0.0 all-to-all-done.near
  51.0 1.9 %collective-permute-start.7 = (bf16[2,2,80,512]{3,2,1,0:T(8,128)(2,1)S(1)}, bf16[2,2,80,512]{3,2,1,0:T(8,128)(2,1)S(1)}, u32[]{:S(2)}, u32[]{:S(2)}) collective-permute-start(bf16[2,2,80,512]{3,2,1,0:T(8,128)(2,1)S(1)} %get-tuple-element.35), channel_id=1, source_target_pairs={{0,7},{1,0},{2,1},{3,2},{4,3},{5,4},{6,5},{7,6},{8,15},{9,8},{10,9... | collective-permute-start | bytes 983048 | tf_op jit(solution)/shard_map/ppermute | solution.py:264
  52.9 3.4 %collective-permute-start.6 = (bf16[2,2,80,512]{3,2,1,0:T(8,128)(2,1)S(1)}, bf16[2,2,80,512]{3,2,1,0:T(8,128)(2,1)S(1)}, u32[]{:S(2)}, u32[]{:S(2)}) collective-permute-start(bf16[2,2,80,512]{3,2,1,0:T(8,128)(2,1)S(1)} %get-tuple-element.36), channel_id=1, source_target_pairs={{0,1},{1,2},{2,3},{3,4},{4,5},{5,6},{6,7},{7,0},{8,9},{9,10},{10,1... | collective-permute-start | bytes 983048 | tf_op jit(solution)/shard_map/ppermute | solution.py:263
  56.3 3.8 %collective-permute-done.7.high = bf16[2,2,80,512]{3,2,1,0:T(8,128)(2,1)S(1)} collective-permute-done((bf16[2,2,80,512]{3,2,1,0:T(8,128)(2,1)S(1)}, bf16[2,2,80,512]{3,2,1,0:T(8,128)(2,1)S(1)}, u32[]{:S(2)}, u32[]{:S(2)}) %collective-permute-start.7) | collective-permute-done | bytes 327712 | tf_op jit(solution)/shard_map/ppermute | solution.py:264
  60.0 1.9 %collective-permute-done.6.low = bf16[2,2,80,512]{3,2,1,0:T(8,128)(2,1)S(1)} collective-permute-done((bf16[2,2,80,512]{3,2,1,0:T(8,128)(2,1)S(1)}, bf16[2,2,80,512]{3,2,1,0:T(8,128)(2,1)S(1)}, u32[]{:S(2)}, u32[]{:S(2)}) %collective-permute-start.6) | collective-permute-done | bytes 327712 | tf_op jit(solution)/shard_map/ppermute | solution.py:263
  62.0 1.7 shard_map.66
  63.6 14.5 %all_to_all.30 = bf16[4,4,2,32,512]{4,3,2,1,0:T(8,128)(2,1)S(1)} all-to-all(bf16[4,4,2,32,512]{4,3,2,1,0:T(8,128)(2,1)S(1)} %shard_map.66), channel_id=1, replica_groups=mesh['zh'=4,'zl'=4,'x'=4,'k'=2,'yh'=4,'yl'=2] {'x'}, dimensions={0} | all-to-all | bytes 2097152 | tf_op jit(solution)/shard_map/all_to_all | solution.py:185
  78.2 0.1 fusion
  78.3 34.0 %all_to_all.31 = bf16[4,2,32,512]{3,2,1,0:T(8,128)(2,1)S(1)} all-to-all(bf16[4,2,32,512]{3,2,1,0:T(8,128)(2,1)S(1)} %fusion), channel_id=1, replica_groups=mesh['zh'=4,'zl'=4,'x'=4,'k'=2,'yh'=4,'yl'=2] {'zh'}, dimensions={0} | all-to-all | bytes 524288 | tf_op jit(solution)/shard_map/all_to_all | solution.py:185
  112.3 0.1 fusion.1
  112.4 17.8 %all_to_all.32 = bf16[4,2,32,512]{3,2,1,0:T(8,128)(2,1)S(1)} all-to-all(bf16[4,2,32,512]{3,2,1,0:T(8,128)(2,1)S(1)} %broadcast_in_dim.4), channel_id=1, replica_groups=mesh['zh'=4,'zl'=4,'x'=4,'k'=2,'yh'=4,'yl'=2] {'zh'}, dimensions={0} | all-to-all | bytes 524288 | tf_op jit(solution)/shard_map/all_to_all | solution.py:185
  130.2 0.1 broadcast_in_dim.5
  130.3 12.7 %all_to_all.33.amp_ref = bf16[4,4,2,32,512]{4,3,2,1,0:T(8,128)(2,1)S(1)} all-to-all(bf16[4,4,2,32,512]{4,3,2,1,0:T(8,128)(2,1)S(1)} %broadcast_in_dim.5), channel_id=1, replica_groups=mesh['zh'=4,'zl'=4,'x'=4,'k'=2,'yh'=4,'yl'=2] {'x'}, dimensions={0} | all-to-all | bytes 2097152 | tf_op jit(solution)/shard_map/all_to_all | solution.py:185
  143.0 1.4 shard_map.67
  144.4 25.4 %all_to_all.34.parts_ref = bf16[4,2,80,512]{3,2,1,0:T(8,128)(2,1)S(1)} all-to-all(bf16[4,2,80,512]{3,2,1,0:T(8,128)(2,1)S(1)} %shard_map.67), channel_id=1, replica_groups=mesh['zh'=4,'zl'=4,'x'=4,'k'=2,'yh'=4,'yl'=2] {'zl'}, dimensions={0} | all-to-all | bytes 1310720 | tf_op jit(solution)/shard_map/all_to_all | solution.py:185
  169.8 4.7 %collective-permute-start.8 = (f32[80,512]{1,0:T(8,128)S(1)}, f32[80,512]{1,0:T(8,128)S(1)}, u32[]{:S(2)}, u32[]{:S(2)}) collective-permute-start(f32[80,512]{1,0:T(8,128)S(1)} %add_bitcast_fusion), channel_id=1, source_target_pairs={{0,8},{8,0},{1,9},{9,1},{2,10},{10,2},{3,11},{11,3},{4,12},{12,4},... | collective-permute-start | bytes 491528 | tf_op jit(solution)/shard_map/ppermute | solution.py:274
  174.5 1.0 collective-permute-done.8.came_ref
  175.5 0.8 shard_map.68
  (4 shorter events, 0.1 us)
Async XLA Ops:
  5.0 17.1 %collective-permute-start = (bf16[80,512]{1,0:T(8,128)(2,1)}, bf16[80,512]{1,0:T(8,128)(2,1)S(1)}, u32[]{:S(2)}, u32[]{:S(2)}) collective-permute-start(bf16[80,512]{1,0:T(8,128)(2,1)} %get-tuple-element.20), channel_id=1, source_target_pairs={{0,0},{1,66},{2,132},{3,198},{4,8},{5,74},{6,140},{7,206},{8,1},{9... | collective-permute-start | bytes 245768 | tf_op jit(solution)/shard_map/ppermute | solution.py:239
  14.7 10.6 %collective-permute-start.1 = (bf16[80,512]{1,0:T(8,128)(2,1)}, bf16[80,512]{1,0:T(8,128)(2,1)S(1)}, u32[]{:S(2)}, u32[]{:S(2)}) collective-permute-start(bf16[80,512]{1,0:T(8,128)(2,1)} %get-tuple-element.21), channel_id=1, source_target_pairs={{0,8},{1,74},{2,140},{3,206},{4,0},{5,66},{6,132},{7,198},{8,9},{9... | collective-permute-start | bytes 245768 | tf_op jit(solution)/shard_map/ppermute | solution.py:239
  16.6 4.6 %collective-permute-start.2 = (bf16[80,512]{1,0:T(8,128)(2,1)}, bf16[80,512]{1,0:T(8,128)(2,1)S(1)}, u32[]{:S(2)}, u32[]{:S(2)}) collective-permute-start(bf16[80,512]{1,0:T(8,128)(2,1)} %get-tuple-element.23), channel_id=1, source_target_pairs={{0,8},{8,0},{1,9},{9,1},{2,10},{10,2},{3,11},{11,3},{4,12},{12,4},... | collective-permute-start | bytes 245768 | tf_op jit(solution)/shard_map/ppermute | solution.py:253
  26.2 24.8 %all-to-all-start = ((bf16[4,2,80,512]{3,2,1,0:T(8,128)(2,1)}), bf16[4,2,80,512]{3,2,1,0:T(8,128)(2,1)S(1)}, u32[]{:S(2)}, u32[]{:S(2)}) async-start(bf16[4,2,80,512]{3,2,1,0:T(8,128)(2,1)} %shard_map.65), calls=%async_computation | async-start | bytes 1310720 | tf_op jit(solution)/shard_map/all_to_all | solution.py:185
  34.8 9.3 %collective-permute-start.5 = (bf16[2,80,512]{2,1,0:T(8,128)(2,1)S(1)}, bf16[2,80,512]{2,1,0:T(8,128)(2,1)S(1)}, u32[]{:S(2)}, u32[]{:S(2)}) collective-permute-start(bf16[2,80,512]{2,1,0:T(8,128)(2,1)S(1)} %pad_maximum_fusion.refs_0_), channel_id=1, source_target_pairs={{0,192},{64,128},{128,64},{192,0},{1,193},{65,129},{129,65},{193,1... | collective-permute-start | bytes 491528 | tf_op jit(solution)/shard_map/ppermute | solution.py:259
  36.8 14.2 %collective-permute-start.4 = (bf16[2,80,512]{2,1,0:T(8,128)(2,1)S(1)}, bf16[2,80,512]{2,1,0:T(8,128)(2,1)S(1)}, u32[]{:S(2)}, u32[]{:S(2)}) collective-permute-start(bf16[2,80,512]{2,1,0:T(8,128)(2,1)S(1)} %pad_maximum_fusion.refs_0_), channel_id=1, source_target_pairs={{0,64},{64,0},{128,192},{192,128},{1,65},{65,1},{129,193},{193,129... | collective-permute-start | bytes 491528 | tf_op jit(solution)/shard_map/ppermute | solution.py:259
  38.7 12.3 %collective-permute-start.3 = (bf16[2,80,512]{2,1,0:T(8,128)(2,1)S(1)}, bf16[2,80,512]{2,1,0:T(8,128)(2,1)S(1)}, u32[]{:S(2)}, u32[]{:S(2)}) collective-permute-start(bf16[2,80,512]{2,1,0:T(8,128)(2,1)S(1)} %pad_maximum_fusion.refs_0_), channel_id=1, source_target_pairs={{0,128},{64,192},{128,0},{192,64},{1,129},{65,193},{129,1},{193,65... | collective-permute-start | bytes 491528 | tf_op jit(solution)/shard_map/ppermute | solution.py:259
  51.0 9.1 %collective-permute-start.7 = (bf16[2,2,80,512]{3,2,1,0:T(8,128)(2,1)S(1)}, bf16[2,2,80,512]{3,2,1,0:T(8,128)(2,1)S(1)}, u32[]{:S(2)}, u32[]{:S(2)}) collective-permute-start(bf16[2,2,80,512]{3,2,1,0:T(8,128)(2,1)S(1)} %get-tuple-element.35), channel_id=1, source_target_pairs={{0,7},{1,0},{2,1},{3,2},{4,3},{5,4},{6,5},{7,6},{8,15},{9,8},{10,9... | collective-permute-start | bytes 983048 | tf_op jit(solution)/shard_map/ppermute | solution.py:264
  52.9 9.1 %collective-permute-start.6 = (bf16[2,2,80,512]{3,2,1,0:T(8,128)(2,1)S(1)}, bf16[2,2,80,512]{3,2,1,0:T(8,128)(2,1)S(1)}, u32[]{:S(2)}, u32[]{:S(2)}) collective-permute-start(bf16[2,2,80,512]{3,2,1,0:T(8,128)(2,1)S(1)} %get-tuple-element.36), channel_id=1, source_target_pairs={{0,1},{1,2},{2,3},{3,4},{4,5},{5,6},{6,7},{7,0},{8,9},{9,10},{10,1... | collective-permute-start | bytes 983048 | tf_op jit(solution)/shard_map/ppermute | solution.py:263
  169.8 5.7 %collective-permute-start.8 = (f32[80,512]{1,0:T(8,128)S(1)}, f32[80,512]{1,0:T(8,128)S(1)}, u32[]{:S(2)}, u32[]{:S(2)}) collective-permute-start(f32[80,512]{1,0:T(8,128)S(1)} %add_bitcast_fusion), channel_id=1, source_target_pairs={{0,8},{8,0},{1,9},{9,1},{2,10},{10,2},{3,11},{11,3},{4,12},{12,4},... | collective-permute-start | bytes 491528 | tf_op jit(solution)/shard_map/ppermute | solution.py:274

commit v5 on v4

--- a/solution.py
+++ b/solution.py
@@ -255,7 +255,7 @@
             (turned, second, denominator, targets, flip)
         )
 
-        near = exchange(copied(turned, high), "yh")
+        near = lax.all_gather(copied(turned, 1)[0], "yh", axis=0, tiled=False)
         others = [lax.ppermute(second, GM, [(m, m ^ d) for m in range(gm)]) for d in (2, 1, 3)]
         near, others = lax.optimization_barrier((near, others))
         second_all = [second, others[1], others[0], others[2]]

time: 177 us -> 174 us (0.983)
  the two profiles are of different devices: /device:TPU:17 before, /device:TPU:1 now
where the time goes in v5:
time: 174 us
  blocking collectives  105 us (60%)
  starting transfers between devices  48.8 us (28%)
  Pallas kernels  8.22 us (5%)
  waiting for transfers between devices  6.68 us (4%)
  other arithmetic  1.9 us (1%)
    all_to_all x5, blocking collectives, exchange(): return lax.all_to_all(parts, axis, 0, 0, tiled=True)  87.8 us
    all_gather x1, blocking collectives, local(): near = lax.all_gather(copied(turned, 1)[0], 'yh', axis=0, tiled=False)  17.6 us
    ppermute x1, starting transfers between devices, local(): return finish(core, dens, lax.ppermute(given, 'k', swap))  14.8 us
    ppermute x3, starting transfers between devices, local(): lax.ppermute(second, GM, [(m, m ^ d) for m in range(gm)])  9.27 us
    ppermute x1, starting transfers between devices, local(): second = jnp.stack([kept, lax.ppermute(given, 'k', swap)])  8.89 us
    ppermute x1, starting transfers between devices, local(): lax.ppermute(turn_b, order, turns[1])  6.03 us
    ppermute x1, starting transfers between devices, local(): lax.ppermute(turn_a, order, turns[0])  4.59 us
    pallas_call x1, Pallas kernels, transform(): pl.pallas_call(kernel, in_specs=[hbm] * 5, out_specs=[vmem] * 4 + [pl.Blo...  4.32 us
  transfers between devices with their start and end apart: 9, of which 3 were waited for; matrix products, arithmetic and copies ran while one was open for 2% of the time, Pallas kernels for 0%

profile of v5, /device:TPU:1, one launch (start us, length us, event | category | flops | bytes accessed | tf_op | source)
XLA Modules:
  0.0 173.6 jit_solution(14617080963149448851)
XLA Ops:
  0.7 4.3 %shard_map.64 = (bf16[80,512]{1,0:T(8,128)(2,1)}, bf16[80,512]{1,0:T(8,128)(2,1)}, bf16[80,512]{1,0:T(8,128)(2,1)}, bf16[80,512]{1,0:T(8,128)(2,1)}, f32[1]{0:T(128)}) custom-call(s32[1]{0:T(128)S(6)} %copy.7.count_hbm, s32[2,2]{1,0:T(2,128)} %pairs_hbm.1, f32[3]{0:T(128)} %energies_hbm.1, bf16[3,80,4608]{2,1,0:T(8,128)(2,1)} %bitcast.18, ...), custom_call_target="tpu_custom_call" | custom-call | tf_op jit(solution)/shard_map/pallas_call | solution.py:72
  5.0 4.6 %collective-permute-start = (bf16[80,512]{1,0:T(8,128)(2,1)}, bf16[80,512]{1,0:T(8,128)(2,1)S(1)}, u32[]{:S(2)}, u32[]{:S(2)}) collective-permute-start(bf16[80,512]{1,0:T(8,128)(2,1)} %get-tuple-element.20), channel_id=1, source_target_pairs={{0,0},{1,66},{2,132},{3,198},{4,8},{5,74},{6,140},{7,206},{8,1},{9... | collective-permute-start | bytes 245768 | tf_op jit(solution)/shard_map/ppermute | solution.py:239
  9.6 6.0 %collective-permute-start.1 = (bf16[80,512]{1,0:T(8,128)(2,1)}, bf16[80,512]{1,0:T(8,128)(2,1)S(1)}, u32[]{:S(2)}, u32[]{:S(2)}) collective-permute-start(bf16[80,512]{1,0:T(8,128)(2,1)} %get-tuple-element.21), channel_id=1, source_target_pairs={{0,8},{1,74},{2,140},{3,206},{4,0},{5,66},{6,132},{7,198},{8,9},{9... | collective-permute-start | bytes 245768 | tf_op jit(solution)/shard_map/ppermute | solution.py:239
  15.6 8.9 %collective-permute-start.2 = (bf16[80,512]{1,0:T(8,128)(2,1)}, bf16[80,512]{1,0:T(8,128)(2,1)S(1)}, u32[]{:S(2)}, u32[]{:S(2)}) collective-permute-start(bf16[80,512]{1,0:T(8,128)(2,1)} %get-tuple-element.23), channel_id=1, source_target_pairs={{0,8},{8,0},{1,9},{9,1},{2,10},{10,2},{3,11},{11,3},{4,12},{12,4},... | collective-permute-start | bytes 245768 | tf_op jit(solution)/shard_map/ppermute | solution.py:253
  24.5 0.8 dynamic_slice.11
  25.3 0.8 dynamic-slice_bitcast_fusion.1
  26.1 0.7 maximum_subtract_fusion
  26.8 0.1 broadcast_subtract_fusion
  26.9 0.0 collective-permute-done.2
  26.9 0.9 pad_maximum_fusion.refs_0_
  27.8 0.0 collective-permute-done.refs_0_
  27.8 0.0 collective-permute-done.1.refs_1_
  27.8 1.9 %collective-permute-start.5 = (bf16[2,80,512]{2,1,0:T(8,128)(2,1)S(1)}, bf16[2,80,512]{2,1,0:T(8,128)(2,1)S(1)}, u32[]{:S(2)}, u32[]{:S(2)}) collective-permute-start(bf16[2,80,512]{2,1,0:T(8,128)(2,1)S(1)} %pad_maximum_fusion.refs_0_), channel_id=1, source_target_pairs={{0,192},{64,128},{128,64},{192,0},{1,193},{65,129},{129,65},{193,1... | collective-permute-start | bytes 491528 | tf_op jit(solution)/shard_map/ppermute | solution.py:259
  29.7 2.3 %collective-permute-start.4 = (bf16[2,80,512]{2,1,0:T(8,128)(2,1)S(1)}, bf16[2,80,512]{2,1,0:T(8,128)(2,1)S(1)}, u32[]{:S(2)}, u32[]{:S(2)}) collective-permute-start(bf16[2,80,512]{2,1,0:T(8,128)(2,1)S(1)} %pad_maximum_fusion.refs_0_), channel_id=1, source_target_pairs={{0,64},{64,0},{128,192},{192,128},{1,65},{65,1},{129,193},{193,129... | collective-permute-start | bytes 491528 | tf_op jit(solution)/shard_map/ppermute | solution.py:259
  32.0 5.1 %collective-permute-start.3 = (bf16[2,80,512]{2,1,0:T(8,128)(2,1)S(1)}, bf16[2,80,512]{2,1,0:T(8,128)(2,1)S(1)}, u32[]{:S(2)}, u32[]{:S(2)}) collective-permute-start(bf16[2,80,512]{2,1,0:T(8,128)(2,1)S(1)} %pad_maximum_fusion.refs_0_), channel_id=1, source_target_pairs={{0,128},{64,192},{128,0},{192,64},{1,129},{65,193},{129,1},{193,65... | collective-permute-start | bytes 491528 | tf_op jit(solution)/shard_map/ppermute | solution.py:259
  37.1 17.6 %all_gather.3.near = bf16[4,2,80,512]{3,2,1,0:T(8,128)(2,1)S(1)} all-gather(bf16[1,2,80,512]{3,2,1,0:T(8,128)(2,1)S(1)} %shard_map.65), channel_id=1, replica_groups=mesh['zh'=4,'zl'=4,'x'=4,'k'=2,'yh'=4,'yl'=2] {'yh'}, dimensions={0}, use_global_device_ids=true | all-gather | bytes 819200 | tf_op jit(solution)/shard_map/all_gather | solution.py:258
  54.7 0.0 collective-permute-done.5.refs_3_
  54.7 0.0 collective-permute-done.4.refs_1_
  54.7 0.0 collective-permute-done.3.refs_2_
  54.8 1.9 %collective-permute-start.7 = (bf16[2,2,80,512]{3,2,1,0:T(8,128)(2,1)S(1)}, bf16[2,2,80,512]{3,2,1,0:T(8,128)(2,1)S(1)}, u32[]{:S(2)}, u32[]{:S(2)}) collective-permute-start(bf16[2,2,80,512]{3,2,1,0:T(8,128)(2,1)S(1)} %get-tuple-element.35), channel_id=1, source_target_pairs={{0,7},{1,0},{2,1},{3,2},{4,3},{5,4},{6,5},{7,6},{8,15},{9,8},{10,9... | collective-permute-start | bytes 983048 | tf_op jit(solution)/shard_map/ppermute | solution.py:264
  56.7 3.4 %collective-permute-start.6 = (bf16[2,2,80,512]{3,2,1,0:T(8,128)(2,1)S(1)}, bf16[2,2,80,512]{3,2,1,0:T(8,128)(2,1)S(1)}, u32[]{:S(2)}, u32[]{:S(2)}) collective-permute-start(bf16[2,2,80,512]{3,2,1,0:T(8,128)(2,1)S(1)} %get-tuple-element.36), channel_id=1, source_target_pairs={{0,1},{1,2},{2,3},{3,4},{4,5},{5,6},{6,7},{7,0},{8,9},{9,10},{10,1... | collective-permute-start | bytes 983048 | tf_op jit(solution)/shard_map/ppermute | solution.py:263
  60.1 2.5 %collective-permute-done.7.high = bf16[2,2,80,512]{3,2,1,0:T(8,128)(2,1)S(1)} collective-permute-done((bf16[2,2,80,512]{3,2,1,0:T(8,128)(2,1)S(1)}, bf16[2,2,80,512]{3,2,1,0:T(8,128)(2,1)S(1)}, u32[]{:S(2)}, u32[]{:S(2)}) %collective-permute-start.7) | collective-permute-done | bytes 327712 | tf_op jit(solution)/shard_map/ppermute | solution.py:264
  62.6 3.1 %collective-permute-done.6.low = bf16[2,2,80,512]{3,2,1,0:T(8,128)(2,1)S(1)} collective-permute-done((bf16[2,2,80,512]{3,2,1,0:T(8,128)(2,1)S(1)}, bf16[2,2,80,512]{3,2,1,0:T(8,128)(2,1)S(1)}, u32[]{:S(2)}, u32[]{:S(2)}) %collective-permute-start.6) | collective-permute-done | bytes 327712 | tf_op jit(solution)/shard_map/ppermute | solution.py:263
  65.7 1.7 shard_map.66
  67.4 12.2 %all_to_all.25 = bf16[4,4,2,32,512]{4,3,2,1,0:T(8,128)(2,1)S(1)} all-to-all(bf16[4,4,2,32,512]{4,3,2,1,0:T(8,128)(2,1)S(1)} %shard_map.66), channel_id=1, replica_groups=mesh['zh'=4,'zl'=4,'x'=4,'k'=2,'yh'=4,'yl'=2] {'x'}, dimensions={0} | all-to-all | bytes 2097152 | tf_op jit(solution)/shard_map/all_to_all | solution.py:185
  79.6 0.1 fusion
  79.7 30.8 %all_to_all.26 = bf16[4,2,32,512]{3,2,1,0:T(8,128)(2,1)S(1)} all-to-all(bf16[4,2,32,512]{3,2,1,0:T(8,128)(2,1)S(1)} %fusion), channel_id=1, replica_groups=mesh['zh'=4,'zl'=4,'x'=4,'k'=2,'yh'=4,'yl'=2] {'zh'}, dimensions={0} | all-to-all | bytes 524288 | tf_op jit(solution)/shard_map/all_to_all | solution.py:185
  110.5 18.2 %all_to_all.27 = bf16[4,2,32,512]{3,2,1,0:T(8,128)(2,1)S(1)} all-to-all(bf16[4,2,32,512]{3,2,1,0:T(8,128)(2,1)S(1)} %broadcast_in_dim.4), channel_id=1, replica_groups=mesh['zh'=4,'zl'=4,'x'=4,'k'=2,'yh'=4,'yl'=2] {'zh'}, dimensions={0} | all-to-all | bytes 524288 | tf_op jit(solution)/shard_map/all_to_all | solution.py:185
  128.7 0.1 broadcast_in_dim.5
  128.9 12.2 %all_to_all.28.amp_ref = bf16[4,4,2,32,512]{4,3,2,1,0:T(8,128)(2,1)S(1)} all-to-all(bf16[4,4,2,32,512]{4,3,2,1,0:T(8,128)(2,1)S(1)} %broadcast_in_dim.5), channel_id=1, replica_groups=mesh['zh'=4,'zl'=4,'x'=4,'k'=2,'yh'=4,'yl'=2] {'x'}, dimensions={0} | all-to-all | bytes 2097152 | tf_op jit(solution)/shard_map/all_to_all | solution.py:185
  141.0 1.4 shard_map.67
  142.4 14.5 %all_to_all.29.parts_ref = bf16[4,2,80,512]{3,2,1,0:T(8,128)(2,1)S(1)} all-to-all(bf16[4,2,80,512]{3,2,1,0:T(8,128)(2,1)S(1)} %shard_map.67), channel_id=1, replica_groups=mesh['zh'=4,'zl'=4,'x'=4,'k'=2,'yh'=4,'yl'=2] {'zl'}, dimensions={0} | all-to-all | bytes 1310720 | tf_op jit(solution)/shard_map/all_to_all | solution.py:185
  157.0 14.8 %collective-permute-start.8 = (f32[80,512]{1,0:T(8,128)S(1)}, f32[80,512]{1,0:T(8,128)S(1)}, u32[]{:S(2)}, u32[]{:S(2)}) collective-permute-start(f32[80,512]{1,0:T(8,128)S(1)} %add_bitcast_fusion), channel_id=1, source_target_pairs={{0,8},{8,0},{1,9},{9,1},{2,10},{10,2},{3,11},{11,3},{4,12},{12,4},... | collective-permute-start | bytes 491528 | tf_op jit(solution)/shard_map/ppermute | solution.py:274
  171.7 1.0 collective-permute-done.8.came_ref
  172.7 0.8 shard_map.68
  (6 shorter events, 0.2 us)
Async XLA Ops:
  5.0 22.8 %collective-permute-start = (bf16[80,512]{1,0:T(8,128)(2,1)}, bf16[80,512]{1,0:T(8,128)(2,1)S(1)}, u32[]{:S(2)}, u32[]{:S(2)}) collective-permute-start(bf16[80,512]{1,0:T(8,128)(2,1)} %get-tuple-element.20), channel_id=1, source_target_pairs={{0,0},{1,66},{2,132},{3,198},{4,8},{5,74},{6,140},{7,206},{8,1},{9... | collective-permute-start | bytes 245768 | tf_op jit(solution)/shard_map/ppermute | solution.py:239
  9.6 18.2 %collective-permute-start.1 = (bf16[80,512]{1,0:T(8,128)(2,1)}, bf16[80,512]{1,0:T(8,128)(2,1)S(1)}, u32[]{:S(2)}, u32[]{:S(2)}) collective-permute-start(bf16[80,512]{1,0:T(8,128)(2,1)} %get-tuple-element.21), channel_id=1, source_target_pairs={{0,8},{1,74},{2,140},{3,206},{4,0},{5,66},{6,132},{7,198},{8,9},{9... | collective-permute-start | bytes 245768 | tf_op jit(solution)/shard_map/ppermute | solution.py:239
  15.6 11.3 %collective-permute-start.2 = (bf16[80,512]{1,0:T(8,128)(2,1)}, bf16[80,512]{1,0:T(8,128)(2,1)S(1)}, u32[]{:S(2)}, u32[]{:S(2)}) collective-permute-start(bf16[80,512]{1,0:T(8,128)(2,1)} %get-tuple-element.23), channel_id=1, source_target_pairs={{0,8},{8,0},{1,9},{9,1},{2,10},{10,2},{3,11},{11,3},{4,12},{12,4},... | collective-permute-start | bytes 245768 | tf_op jit(solution)/shard_map/ppermute | solution.py:253
  27.8 26.9 %collective-permute-start.5 = (bf16[2,80,512]{2,1,0:T(8,128)(2,1)S(1)}, bf16[2,80,512]{2,1,0:T(8,128)(2,1)S(1)}, u32[]{:S(2)}, u32[]{:S(2)}) collective-permute-start(bf16[2,80,512]{2,1,0:T(8,128)(2,1)S(1)} %pad_maximum_fusion.refs_0_), channel_id=1, source_target_pairs={{0,192},{64,128},{128,64},{192,0},{1,193},{65,129},{129,65},{193,1... | collective-permute-start | bytes 491528 | tf_op jit(solution)/shard_map/ppermute | solution.py:259
  29.7 25.0 %collective-permute-start.4 = (bf16[2,80,512]{2,1,0:T(8,128)(2,1)S(1)}, bf16[2,80,512]{2,1,0:T(8,128)(2,1)S(1)}, u32[]{:S(2)}, u32[]{:S(2)}) collective-permute-start(bf16[2,80,512]{2,1,0:T(8,128)(2,1)S(1)} %pad_maximum_fusion.refs_0_), channel_id=1, source_target_pairs={{0,64},{64,0},{128,192},{192,128},{1,65},{65,1},{129,193},{193,129... | collective-permute-start | bytes 491528 | tf_op jit(solution)/shard_map/ppermute | solution.py:259
  32.0 22.7 %collective-permute-start.3 = (bf16[2,80,512]{2,1,0:T(8,128)(2,1)S(1)}, bf16[2,80,512]{2,1,0:T(8,128)(2,1)S(1)}, u32[]{:S(2)}, u32[]{:S(2)}) collective-permute-start(bf16[2,80,512]{2,1,0:T(8,128)(2,1)S(1)} %pad_maximum_fusion.refs_0_), channel_id=1, source_target_pairs={{0,128},{64,192},{128,0},{192,64},{1,129},{65,193},{129,1},{193,65... | collective-permute-start | bytes 491528 | tf_op jit(solution)/shard_map/ppermute | solution.py:259
  54.8 7.8 %collective-permute-start.7 = (bf16[2,2,80,512]{3,2,1,0:T(8,128)(2,1)S(1)}, bf16[2,2,80,512]{3,2,1,0:T(8,128)(2,1)S(1)}, u32[]{:S(2)}, u32[]{:S(2)}) collective-permute-start(bf16[2,2,80,512]{3,2,1,0:T(8,128)(2,1)S(1)} %get-tuple-element.35), channel_id=1, source_target_pairs={{0,7},{1,0},{2,1},{3,2},{4,3},{5,4},{6,5},{7,6},{8,15},{9,8},{10,9... | collective-permute-start | bytes 983048 | tf_op jit(solution)/shard_map/ppermute | solution.py:264
  56.7 9.0 %collective-permute-start.6 = (bf16[2,2,80,512]{3,2,1,0:T(8,128)(2,1)S(1)}, bf16[2,2,80,512]{3,2,1,0:T(8,128)(2,1)S(1)}, u32[]{:S(2)}, u32[]{:S(2)}) collective-permute-start(bf16[2,2,80,512]{3,2,1,0:T(8,128)(2,1)S(1)} %get-tuple-element.36), channel_id=1, source_target_pairs={{0,1},{1,2},{2,3},{3,4},{4,5},{5,6},{6,7},{7,0},{8,9},{9,10},{10,1... | collective-permute-start | bytes 983048 | tf_op jit(solution)/shard_map/ppermute | solution.py:263
  157.0 15.8 %collective-permute-start.8 = (f32[80,512]{1,0:T(8,128)S(1)}, f32[80,512]{1,0:T(8,128)S(1)}, u32[]{:S(2)}, u32[]{:S(2)}) collective-permute-start(f32[80,512]{1,0:T(8,128)S(1)} %add_bitcast_fusion), channel_id=1, source_target_pairs={{0,8},{8,0},{1,9},{9,1},{2,10},{10,2},{3,11},{11,3},{4,12},{12,4},... | collective-permute-start | bytes 491528 | tf_op jit(solution)/shard_map/ppermute | solution.py:274

commit v6 on v5

--- a/solution.py
+++ b/solution.py
@@ -102,7 +102,8 @@
         held = [flat(near), jnp.concatenate([flat(low), flat(high)], axis=0)]
         for k in range(2):
             at = side_ref[0] if k == 0 else 1 - side_ref[0]
-            b = jnp.concatenate([r[at] for r in refs[:-1]], axis=0)
+            own, across, beside = refs[:-1]
+            b = jnp.concatenate([own[at], beside[0, at], across[at], beside[1, at]], axis=0)
             value += lax.dot_general(
                 held[k], b, (((0,), (0,)), ((), ())), preferred_element_type=f32
             )
@@ -113,7 +114,7 @@
         grid=(halves,),
         in_specs=[pl.BlockSpec(memory_space=pltpu.SMEM)]
         + [pl.BlockSpec((f.shape[0], 1, slots, width), lambda h: (0, h, 0, 0)) for f in first]
-        + [pl.BlockSpec(r.shape, lambda h: (0, 0, 0)) for r in second],
+        + [pl.BlockSpec(r.shape, lambda h, n=r.ndim: (0,) * n) for r in second],
         out_specs=pl.BlockSpec((n1, n2, 1, piece, width), lambda h: (0, 0, h, 0, 0)),
         out_shape=jax.ShapeDtypeStruct((n1, n2, halves, piece, width), bf16),
         compiler_params=params(),
@@ -256,9 +257,11 @@
         )
 
         near = lax.all_gather(copied(turned, 1)[0], "yh", axis=0, tiled=False)
-        others = [lax.ppermute(second, GM, [(m, m ^ d) for m in range(gm)]) for d in (2, 1, 3)]
-        near, others = lax.optimization_barrier((near, others))
-        second_all = [second, others[1], others[0], others[2]]
+        across = lax.ppermute(second, GM, [(m, m ^ 2) for m in range(gm)])
+        near, across = lax.optimization_barrier((near, across))
+        held = jnp.stack([second, across])
+        beside = lax.ppermute(held, GM, [(m, m ^ 1) for m in range(gm)])
+        second_all = [second, across, beside]
         middle = high // 2
         far_low = lax.ppermute(near[:middle], ("yh", "yl"), up)
         far_high = lax.ppermute(near[middle:], ("yh", "yl"), down)

time: 174 us -> 172 us (0.989)
  starting transfers between devices: 48.8 us -> 44.1 us
  blocking collectives: 105 us -> 107 us
    ppermute x3 -> x2, starting transfers between devices: 9.27 us -> 4.41 us  [the longest x1 2.49 us: local(): beside = lax.ppermute(held, GM, [(m, m ^ 1) for m in range(gm)])]
  transfers between devices with their start and end apart: 9 -> 8, of which waited for: 3 -> 4; matrix products, arithmetic and copies ran while one was open for 2% -> 2% of each run, Pallas kernels for 0% -> 0%
where the time goes in v6:
time: 172 us; the launch traced here: 171 us
  blocking collectives  107 us (62%)
  starting transfers between devices  44.1 us (26%)
  Pallas kernels  8.2 us (5%)
  waiting for transfers between devices  7.25 us (4%)
  other arithmetic  1.83 us (1%)
  local copies, waits for them, and re-layouts  1.72 us (1%)
    all_to_all x5, blocking collectives, exchange(): return lax.all_to_all(parts, axis, 0, 0, tiled=True)  89.1 us
    all_gather x1, blocking collectives, local(): near = lax.all_gather(copied(turned, 1)[0], 'yh', axis=0, tiled=False)  18.2 us
    ppermute x1, starting transfers between devices, local(): return finish(core, dens, lax.ppermute(given, 'k', swap))  14.8 us
    ppermute x1, starting transfers between devices, local(): second = jnp.stack([kept, lax.ppermute(given, 'k', swap)])  8.89 us
    ppermute x1, starting transfers between devices, local(): lax.ppermute(turn_b, order, turns[1])  6.03 us
    ppermute x1, starting transfers between devices, local(): lax.ppermute(turn_a, order, turns[0])  4.59 us
    pallas_call x1, Pallas kernels, transform(): pl.pallas_call(kernel, in_specs=[hbm] * 5, out_specs=[vmem] * 4 + [pl.Blo...  4.3 us
  transfers between devices with their start and end apart: 8, of which 4 were waited for; matrix products, arithmetic and copies ran while one was open for 2% of the time, Pallas kernels for 0%

profile of v6, /device:TPU:1, one launch (start us, length us, event | category | flops | bytes accessed | tf_op | source)
XLA Modules:
  0.0 171.2 jit_solution(6101674869198019574)
XLA Ops:
  0.7 4.3 %shard_map.64 = (bf16[80,512]{1,0:T(8,128)(2,1)}, bf16[80,512]{1,0:T(8,128)(2,1)}, bf16[80,512]{1,0:T(8,128)(2,1)}, bf16[80,512]{1,0:T(8,128)(2,1)}, f32[1]{0:T(128)}) custom-call(s32[1]{0:T(128)S(6)} %copy.7.count_hbm, s32[2,2]{1,0:T(2,128)} %pairs_hbm.1, f32[3]{0:T(128)} %energies_hbm.1, bf16[3,80,4608]{2,1,0:T(8,128)(2,1)} %bitcast.22, ...), custom_call_target="tpu_custom_call" | custom-call | tf_op jit(solution)/shard_map/pallas_call | solution.py:72
  5.0 4.6 %collective-permute-start = (bf16[80,512]{1,0:T(8,128)(2,1)}, bf16[80,512]{1,0:T(8,128)(2,1)S(1)}, u32[]{:S(2)}, u32[]{:S(2)}) collective-permute-start(bf16[80,512]{1,0:T(8,128)(2,1)} %get-tuple-element.18), channel_id=1, source_target_pairs={{0,0},{1,66},{2,132},{3,198},{4,8},{5,74},{6,140},{7,206},{8,1},{9... | collective-permute-start | bytes 245768 | tf_op jit(solution)/shard_map/ppermute | solution.py:240
  9.6 6.0 %collective-permute-start.1 = (bf16[80,512]{1,0:T(8,128)(2,1)}, bf16[80,512]{1,0:T(8,128)(2,1)S(1)}, u32[]{:S(2)}, u32[]{:S(2)}) collective-permute-start(bf16[80,512]{1,0:T(8,128)(2,1)} %get-tuple-element.19), channel_id=1, source_target_pairs={{0,8},{1,74},{2,140},{3,206},{4,0},{5,66},{6,132},{7,198},{8,9},{9... | collective-permute-start | bytes 245768 | tf_op jit(solution)/shard_map/ppermute | solution.py:240
  15.6 8.9 %collective-permute-start.2 = (bf16[80,512]{1,0:T(8,128)(2,1)}, bf16[80,512]{1,0:T(8,128)(2,1)S(1)}, u32[]{:S(2)}, u32[]{:S(2)}) collective-permute-start(bf16[80,512]{1,0:T(8,128)(2,1)} %get-tuple-element.21), channel_id=1, source_target_pairs={{0,8},{8,0},{1,9},{9,1},{2,10},{10,2},{3,11},{11,3},{4,12},{12,4},... | collective-permute-start | bytes 245768 | tf_op jit(solution)/shard_map/ppermute | solution.py:254
  24.5 0.8 dynamic_slice.11
  25.3 0.8 dynamic-slice_bitcast_fusion.1
  26.1 0.6 maximum_subtract_fusion
  26.6 0.1 broadcast_subtract_fusion
  26.7 0.0 collective-permute-done.2
  26.8 0.9 pad_maximum_fusion.1.refs_0_
  27.7 0.0 collective-permute-done.refs_0_
  27.7 0.0 collective-permute-done.1.refs_1_
  27.7 1.9 %collective-permute-start.3 = (bf16[2,80,512]{2,1,0:T(8,128)(2,1)S(1)}, bf16[2,80,512]{2,1,0:T(8,128)(2,1)S(1)}, u32[]{:S(2)}, u32[]{:S(2)}) collective-permute-start(bf16[2,80,512]{2,1,0:T(8,128)(2,1)S(1)} %pad_maximum_fusion.1.refs_0_), channel_id=1, source_target_pairs={{0,128},{64,192},{128,0},{192,64},{1,129},{65,193},{129,1},{193,65... | collective-permute-start | bytes 491528 | tf_op jit(solution)/shard_map/ppermute | solution.py:260
  29.6 18.2 %all_gather.3.near = bf16[4,2,80,512]{3,2,1,0:T(8,128)(2,1)S(1)} all-gather(bf16[1,2,80,512]{3,2,1,0:T(8,128)(2,1)S(1)} %shard_map.65), channel_id=1, replica_groups=mesh['zh'=4,'zl'=4,'x'=4,'k'=2,'yh'=4,'yl'=2] {'yh'}, dimensions={0}, use_global_device_ids=true | all-gather | bytes 819200 | tf_op jit(solution)/shard_map/all_gather | solution.py:259
  47.8 0.0 collective-permute-done.3.refs_1_
  47.8 2.5 %collective-permute-start.6 = (bf16[2,2,80,512]{3,2,1,0:T(8,128)(2,1)S(1)}, bf16[2,2,80,512]{3,2,1,0:T(8,128)(2,1)S(1)}, u32[]{:S(2)}, u32[]{:S(2)}) collective-permute-start(bf16[2,2,80,512]{3,2,1,0:T(8,128)(2,1)S(1)} %pad_maximum_fusion), channel_id=1, source_target_pairs={{0,64},{64,0},{128,192},{192,128},{1,65},{65,1},{129,193},{193,129... | collective-permute-start | bytes 983048 | tf_op jit(solution)/shard_map/ppermute | solution.py:263
  50.4 2.6 %collective-permute-start.5 = (bf16[2,2,80,512]{3,2,1,0:T(8,128)(2,1)S(1)}, bf16[2,2,80,512]{3,2,1,0:T(8,128)(2,1)S(1)}, u32[]{:S(2)}, u32[]{:S(2)}) collective-permute-start(bf16[2,2,80,512]{3,2,1,0:T(8,128)(2,1)S(1)} %get-tuple-element.31), channel_id=1, source_target_pairs={{0,7},{1,0},{2,1},{3,2},{4,3},{5,4},{6,5},{7,6},{8,15},{9,8},{10,9... | collective-permute-start | bytes 983048 | tf_op jit(solution)/shard_map/ppermute | solution.py:267
  52.9 2.8 %collective-permute-start.4 = (bf16[2,2,80,512]{3,2,1,0:T(8,128)(2,1)S(1)}, bf16[2,2,80,512]{3,2,1,0:T(8,128)(2,1)S(1)}, u32[]{:S(2)}, u32[]{:S(2)}) collective-permute-start(bf16[2,2,80,512]{3,2,1,0:T(8,128)(2,1)S(1)} %get-tuple-element.32), channel_id=1, source_target_pairs={{0,1},{1,2},{2,3},{3,4},{4,5},{5,6},{6,7},{7,0},{8,9},{9,10},{10,1... | collective-permute-start | bytes 983048 | tf_op jit(solution)/shard_map/ppermute | solution.py:266
  55.7 0.9 collective-permute-done.6.refs_2_
  56.6 1.9 %collective-permute-done.5.high = bf16[2,2,80,512]{3,2,1,0:T(8,128)(2,1)S(1)} collective-permute-done((bf16[2,2,80,512]{3,2,1,0:T(8,128)(2,1)S(1)}, bf16[2,2,80,512]{3,2,1,0:T(8,128)(2,1)S(1)}, u32[]{:S(2)}, u32[]{:S(2)}) %collective-permute-start.5) | collective-permute-done | bytes 327712 | tf_op jit(solution)/shard_map/ppermute | solution.py:267
  58.6 3.4 %collective-permute-done.4.low = bf16[2,2,80,512]{3,2,1,0:T(8,128)(2,1)S(1)} collective-permute-done((bf16[2,2,80,512]{3,2,1,0:T(8,128)(2,1)S(1)}, bf16[2,2,80,512]{3,2,1,0:T(8,128)(2,1)S(1)}, u32[]{:S(2)}, u32[]{:S(2)}) %collective-permute-start.4) | collective-permute-done | bytes 327712 | tf_op jit(solution)/shard_map/ppermute | solution.py:266
  62.0 1.7 shard_map.66
  63.7 13.5 %all_to_all.25 = bf16[4,4,2,32,512]{4,3,2,1,0:T(8,128)(2,1)S(1)} all-to-all(bf16[4,4,2,32,512]{4,3,2,1,0:T(8,128)(2,1)S(1)} %shard_map.66), channel_id=1, replica_groups=mesh['zh'=4,'zl'=4,'x'=4,'k'=2,'yh'=4,'yl'=2] {'x'}, dimensions={0} | all-to-all | bytes 2097152 | tf_op jit(solution)/shard_map/all_to_all | solution.py:186
  77.1 0.1 fusion
  77.3 30.4 %all_to_all.26 = bf16[4,2,32,512]{3,2,1,0:T(8,128)(2,1)S(1)} all-to-all(bf16[4,2,32,512]{3,2,1,0:T(8,128)(2,1)S(1)} %fusion), channel_id=1, replica_groups=mesh['zh'=4,'zl'=4,'x'=4,'k'=2,'yh'=4,'yl'=2] {'zh'}, dimensions={0} | all-to-all | bytes 524288 | tf_op jit(solution)/shard_map/all_to_all | solution.py:186
  107.8 18.5 %all_to_all.27 = bf16[4,2,32,512]{3,2,1,0:T(8,128)(2,1)S(1)} all-to-all(bf16[4,2,32,512]{3,2,1,0:T(8,128)(2,1)S(1)} %broadcast_in_dim.4), channel_id=1, replica_groups=mesh['zh'=4,'zl'=4,'x'=4,'k'=2,'yh'=4,'yl'=2] {'zh'}, dimensions={0} | all-to-all | bytes 524288 | tf_op jit(solution)/shard_map/all_to_all | solution.py:186
  126.3 0.1 broadcast_in_dim.5
  126.4 12.2 %all_to_all.28.amp_ref = bf16[4,4,2,32,512]{4,3,2,1,0:T(8,128)(2,1)S(1)} all-to-all(bf16[4,4,2,32,512]{4,3,2,1,0:T(8,128)(2,1)S(1)} %broadcast_in_dim.5), channel_id=1, replica_groups=mesh['zh'=4,'zl'=4,'x'=4,'k'=2,'yh'=4,'yl'=2] {'x'}, dimensions={0} | all-to-all | bytes 2097152 | tf_op jit(solution)/shard_map/all_to_all | solution.py:186
  138.6 1.4 shard_map.67
  140.0 14.5 %all_to_all.29.parts_ref = bf16[4,2,80,512]{3,2,1,0:T(8,128)(2,1)S(1)} all-to-all(bf16[4,2,80,512]{3,2,1,0:T(8,128)(2,1)S(1)} %shard_map.67), channel_id=1, replica_groups=mesh['zh'=4,'zl'=4,'x'=4,'k'=2,'yh'=4,'yl'=2] {'zl'}, dimensions={0} | all-to-all | bytes 1310720 | tf_op jit(solution)/shard_map/all_to_all | solution.py:186
  154.6 14.8 %collective-permute-start.7 = (f32[80,512]{1,0:T(8,128)S(1)}, f32[80,512]{1,0:T(8,128)S(1)}, u32[]{:S(2)}, u32[]{:S(2)}) collective-permute-start(f32[80,512]{1,0:T(8,128)S(1)} %add_bitcast_fusion), channel_id=1, source_target_pairs={{0,8},{8,0},{1,9},{9,1},{2,10},{10,2},{3,11},{11,3},{4,12},{12,4},... | collective-permute-start | bytes 491528 | tf_op jit(solution)/shard_map/ppermute | solution.py:277
  169.4 1.0 collective-permute-done.7.came_ref
  170.4 0.8 shard_map.68
  (7 shorter events, 0.2 us)
Async XLA Ops:
  5.0 22.7 %collective-permute-start = (bf16[80,512]{1,0:T(8,128)(2,1)}, bf16[80,512]{1,0:T(8,128)(2,1)S(1)}, u32[]{:S(2)}, u32[]{:S(2)}) collective-permute-start(bf16[80,512]{1,0:T(8,128)(2,1)} %get-tuple-element.18), channel_id=1, source_target_pairs={{0,0},{1,66},{2,132},{3,198},{4,8},{5,74},{6,140},{7,206},{8,1},{9... | collective-permute-start | bytes 245768 | tf_op jit(solution)/shard_map/ppermute | solution.py:240
  9.6 18.1 %collective-permute-start.1 = (bf16[80,512]{1,0:T(8,128)(2,1)}, bf16[80,512]{1,0:T(8,128)(2,1)S(1)}, u32[]{:S(2)}, u32[]{:S(2)}) collective-permute-start(bf16[80,512]{1,0:T(8,128)(2,1)} %get-tuple-element.19), channel_id=1, source_target_pairs={{0,8},{1,74},{2,140},{3,206},{4,0},{5,66},{6,132},{7,198},{8,9},{9... | collective-permute-start | bytes 245768 | tf_op jit(solution)/shard_map/ppermute | solution.py:240
  15.6 11.1 %collective-permute-start.2 = (bf16[80,512]{1,0:T(8,128)(2,1)}, bf16[80,512]{1,0:T(8,128)(2,1)S(1)}, u32[]{:S(2)}, u32[]{:S(2)}) collective-permute-start(bf16[80,512]{1,0:T(8,128)(2,1)} %get-tuple-element.21), channel_id=1, source_target_pairs={{0,8},{8,0},{1,9},{9,1},{2,10},{10,2},{3,11},{11,3},{4,12},{12,4},... | collective-permute-start | bytes 245768 | tf_op jit(solution)/shard_map/ppermute | solution.py:254
  27.7 20.1 %collective-permute-start.3 = (bf16[2,80,512]{2,1,0:T(8,128)(2,1)S(1)}, bf16[2,80,512]{2,1,0:T(8,128)(2,1)S(1)}, u32[]{:S(2)}, u32[]{:S(2)}) collective-permute-start(bf16[2,80,512]{2,1,0:T(8,128)(2,1)S(1)} %pad_maximum_fusion.1.refs_0_), channel_id=1, source_target_pairs={{0,128},{64,192},{128,0},{192,64},{1,129},{65,193},{129,1},{193,65... | collective-permute-start | bytes 491528 | tf_op jit(solution)/shard_map/ppermute | solution.py:260
  47.8 8.8 %collective-permute-start.6 = (bf16[2,2,80,512]{3,2,1,0:T(8,128)(2,1)S(1)}, bf16[2,2,80,512]{3,2,1,0:T(8,128)(2,1)S(1)}, u32[]{:S(2)}, u32[]{:S(2)}) collective-permute-start(bf16[2,2,80,512]{3,2,1,0:T(8,128)(2,1)S(1)} %pad_maximum_fusion), channel_id=1, source_target_pairs={{0,64},{64,0},{128,192},{192,128},{1,65},{65,1},{129,193},{193,129... | collective-permute-start | bytes 983048 | tf_op jit(solution)/shard_map/ppermute | solution.py:263
  50.4 8.2 %collective-permute-start.5 = (bf16[2,2,80,512]{3,2,1,0:T(8,128)(2,1)S(1)}, bf16[2,2,80,512]{3,2,1,0:T(8,128)(2,1)S(1)}, u32[]{:S(2)}, u32[]{:S(2)}) collective-permute-start(bf16[2,2,80,512]{3,2,1,0:T(8,128)(2,1)S(1)} %get-tuple-element.31), channel_id=1, source_target_pairs={{0,7},{1,0},{2,1},{3,2},{4,3},{5,4},{6,5},{7,6},{8,15},{9,8},{10,9... | collective-permute-start | bytes 983048 | tf_op jit(solution)/shard_map/ppermute | solution.py:267
  52.9 9.0 %collective-permute-start.4 = (bf16[2,2,80,512]{3,2,1,0:T(8,128)(2,1)S(1)}, bf16[2,2,80,512]{3,2,1,0:T(8,128)(2,1)S(1)}, u32[]{:S(2)}, u32[]{:S(2)}) collective-permute-start(bf16[2,2,80,512]{3,2,1,0:T(8,128)(2,1)S(1)} %get-tuple-element.32), channel_id=1, source_target_pairs={{0,1},{1,2},{2,3},{3,4},{4,5},{5,6},{6,7},{7,0},{8,9},{9,10},{10,1... | collective-permute-start | bytes 983048 | tf_op jit(solution)/shard_map/ppermute | solution.py:266
  154.6 15.8 %collective-permute-start.7 = (f32[80,512]{1,0:T(8,128)S(1)}, f32[80,512]{1,0:T(8,128)S(1)}, u32[]{:S(2)}, u32[]{:S(2)}) collective-permute-start(f32[80,512]{1,0:T(8,128)S(1)} %add_bitcast_fusion), channel_id=1, source_target_pairs={{0,8},{8,0},{1,9},{9,1},{2,10},{10,2},{3,11},{11,3},{4,12},{12,4},... | collective-permute-start | bytes 491528 | tf_op jit(solution)/shard_map/ppermute | solution.py:277

commit v7 on v6

--- a/solution.py
+++ b/solution.py
@@ -186,21 +186,27 @@
     return lax.all_to_all(parts, axis, 0, 0, tiled=True)
 
 
-def copied(parts, count):
-    def kernel(*refs):
+def copied(parts, more, count):
+    shape = parts[0].shape
+
+    def kernel(a, b, c, d, copies_ref, more_ref):
         for n in range(count):
-            for i, part in enumerate(refs[:-1]):
-                refs[-1][n, i] = part[...]
-
-    vmem = pl.BlockSpec(memory_space=pltpu.VMEM)
-    shape = (count, len(parts)) + parts[0].shape
-    return pl.pallas_call(
-        kernel,
-        in_specs=[vmem] * len(parts),
-        out_specs=vmem,
-        out_shape=jax.ShapeDtypeStruct(shape, parts[0].dtype),
-        compiler_params=params(),
-    )(*parts)
+            copies_ref[n, 0] = a[...]
+            copies_ref[n, 1] = b[...]
+        more_ref[0] = c[...]
+        more_ref[1] = d[...]
+
+    vmem = pl.BlockSpec(memory_space=pltpu.VMEM)
+    return pl.pallas_call(
+        kernel,
+        in_specs=[vmem] * 4,
+        out_specs=[vmem] * 2,
+        out_shape=[
+            jax.ShapeDtypeStruct((count, 2) + shape, bf16),
+            jax.ShapeDtypeStruct((2,) + shape, bf16),
+        ],
+        compiler_params=params(),
+    )(*parts, *more)
 
 
 def spread(part, axis):
@@ -251,12 +257,8 @@
         denominator = energy[0] - first_vir[:, :, None] - second_vir
         targets = group ^ jnp.arange(gm, dtype=jnp.int32)
         flip = (side ^ core).astype(jnp.int32).reshape(1)
-        second = jnp.stack([kept, lax.ppermute(given, "k", swap)])
-        turned, second, denominator, targets, flip = lax.optimization_barrier(
-            (turned, second, denominator, targets, flip)
-        )
-
-        near = lax.all_gather(copied(turned, 1)[0], "yh", axis=0, tiled=False)
+        copies, second = copied(turned, [kept, lax.ppermute(given, "k", swap)], 1)
+        near = lax.all_gather(copies[0], "yh", axis=0, tiled=False)
         across = lax.ppermute(second, GM, [(m, m ^ 2) for m in range(gm)])
         near, across = lax.optimization_barrier((near, across))
         held = jnp.stack([second, across])
@@ -265,6 +267,9 @@
         middle = high // 2
         far_low = lax.ppermute(near[:middle], ("yh", "yl"), up)
         far_high = lax.ppermute(near[middle:], ("yh", "yl"), down)
+        far_low, far_high, denominator, targets, flip = lax.optimization_barrier(
+            (far_low, far_high, denominator, targets, flip)
+        )
         first_all = [near, far_low, far_high]
 
         parts = coulomb_parts(flip, first_all, second_all, n1, n2)

time: 172 us -> 173 us (level)
  transfers between devices with their start and end apart: 8 -> 8, of which waited for: 4 -> 3; matrix products, arithmetic and copies ran while one was open for 2% -> 1% of each run, Pallas kernels for 0% -> 0%
where the time goes in v7:
time: 173 us; the launch traced here: 172 us
  blocking collectives  107 us (62%)
  starting transfers between devices  45.3 us (26%)
  Pallas kernels  8.19 us (5%)
  waiting for transfers between devices  7.16 us (4%)
  local copies, waits for them, and re-layouts  2.6 us (2%)
    all_to_all x5, blocking collectives, exchange(): return lax.all_to_all(parts, axis, 0, 0, tiled=True)  89.1 us
    all_gather x1, blocking collectives, local(): near = lax.all_gather(copies[0], 'yh', axis=0, tiled=False)  17.8 us
    ppermute x1, starting transfers between devices, local(): return finish(core, dens, lax.ppermute(given, 'k', swap))  14.8 us
    ppermute x1, starting transfers between devices, local(): copies, second = copied(turned, [kept, lax.ppermute(given, 'k', swap)], 1)  8.89 us
    ppermute x1, starting transfers between devices, local(): lax.ppermute(turn_b, order, turns[1])  6.03 us
    ppermute x1, starting transfers between devices, local(): lax.ppermute(turn_a, order, turns[0])  4.59 us
    pallas_call x1, Pallas kernels, transform(): pl.pallas_call(kernel, in_specs=[hbm] * 5, out_specs=[vmem] * 4 + [pl.Blo...  4.3 us
    ppermute x1, starting transfers between devices, local(): beside = lax.ppermute(held, GM, [(m, m ^ 1) for m in range(gm)])  3.76 us
  transfers between devices with their start and end apart: 8, of which 3 were waited for; matrix products, arithmetic and copies ran while one was open for 1% of the time, Pallas kernels for 0%

profile of v7, /device:TPU:1, one launch (start us, length us, event | category | flops | bytes accessed | tf_op | source)
XLA Modules:
  0.0 172.1 jit_solution(17407329358538438537)
XLA Ops:
  0.7 4.3 %shard_map.64 = (bf16[80,512]{1,0:T(8,128)(2,1)}, bf16[80,512]{1,0:T(8,128)(2,1)}, bf16[80,512]{1,0:T(8,128)(2,1)}, bf16[80,512]{1,0:T(8,128)(2,1)}, f32[1]{0:T(128)}) custom-call(s32[1]{0:T(128)S(6)} %copy.7.count_hbm, s32[2,2]{1,0:T(2,128)} %pairs_hbm.1, f32[3]{0:T(128)} %energies_hbm.1, bf16[3,80,4608]{2,1,0:T(8,128)(2,1)} %bitcast.20, ...), custom_call_target="tpu_custom_call" | custom-call | tf_op jit(solution)/shard_map/pallas_call | solution.py:72
  5.0 4.6 %collective-permute-start = (bf16[80,512]{1,0:T(8,128)(2,1)}, bf16[80,512]{1,0:T(8,128)(2,1)S(1)}, u32[]{:S(2)}, u32[]{:S(2)}) collective-permute-start(bf16[80,512]{1,0:T(8,128)(2,1)} %get-tuple-element.19), channel_id=1, source_target_pairs={{0,0},{1,66},{2,132},{3,198},{4,8},{5,74},{6,140},{7,206},{8,1},{9... | collective-permute-start | bytes 245768 | tf_op jit(solution)/shard_map/ppermute | solution.py:246
  9.6 6.0 %collective-permute-start.1 = (bf16[80,512]{1,0:T(8,128)(2,1)}, bf16[80,512]{1,0:T(8,128)(2,1)S(1)}, u32[]{:S(2)}, u32[]{:S(2)}) collective-permute-start(bf16[80,512]{1,0:T(8,128)(2,1)} %get-tuple-element.20), channel_id=1, source_target_pairs={{0,8},{1,74},{2,140},{3,206},{4,0},{5,66},{6,132},{7,198},{8,9},{9... | collective-permute-start | bytes 245768 | tf_op jit(solution)/shard_map/ppermute | solution.py:246
  15.6 8.9 %collective-permute-start.2 = (bf16[80,512]{1,0:T(8,128)(2,1)}, bf16[80,512]{1,0:T(8,128)(2,1)S(1)}, u32[]{:S(2)}, u32[]{:S(2)}) collective-permute-start(bf16[80,512]{1,0:T(8,128)(2,1)} %get-tuple-element.22), channel_id=1, source_target_pairs={{0,8},{8,0},{1,9},{9,1},{2,10},{10,2},{3,11},{11,3},{4,12},{12,4},... | collective-permute-start | bytes 245768 | tf_op jit(solution)/shard_map/ppermute | solution.py:260
  24.5 0.8 dynamic_slice.11
  25.3 0.8 dynamic-slice_bitcast_fusion.1
  26.1 0.7 maximum_subtract_fusion
  26.8 0.0 collective-permute-done.a
  26.8 0.0 collective-permute-done.1.b
  26.8 0.0 collective-permute-done.2.d
  26.8 0.0 copy-start
  26.8 0.9 copy-done
  27.7 1.9 %collective-permute-start.3 = (bf16[2,80,512]{2,1,0:T(8,128)(2,1)S(1)}, bf16[2,80,512]{2,1,0:T(8,128)(2,1)S(1)}, u32[]{:S(2)}, u32[]{:S(2)}) collective-permute-start(bf16[2,80,512]{2,1,0:T(8,128)(2,1)S(1)} %get-tuple-element.24.refs_0_), channel_id=1, source_target_pairs={{0,128},{64,192},{128,0},{192,64},{1,129},{65,193},{129,1},{193,65... | collective-permute-start | bytes 491528 | tf_op jit(solution)/shard_map/ppermute | solution.py:262
  29.6 17.8 %all_gather.3.near = bf16[4,2,80,512]{3,2,1,0:T(8,128)(2,1)S(1)} all-gather(bf16[1,2,80,512]{3,2,1,0:T(8,128)(2,1)S(1)} %get-tuple-element.23), channel_id=1, replica_groups=mesh['zh'=4,'zl'=4,'x'=4,'k'=2,'yh'=4,'yl'=2] {'yh'}, dimensions={0}, use_global_device_ids=true | all-gather | bytes 819200 | tf_op jit(solution)/shard_map/all_gather | solution.py:261
  47.4 0.0 collective-permute-done.3.refs_1_
  47.5 3.8 %collective-permute-start.6 = (bf16[2,2,80,512]{3,2,1,0:T(8,128)(2,1)S(1)}, bf16[2,2,80,512]{3,2,1,0:T(8,128)(2,1)S(1)}, u32[]{:S(2)}, u32[]{:S(2)}) collective-permute-start(bf16[2,2,80,512]{3,2,1,0:T(8,128)(2,1)S(1)} %pad_maximum_fusion), channel_id=1, source_target_pairs={{0,64},{64,0},{128,192},{192,128},{1,65},{65,1},{129,193},{193,129... | collective-permute-start | bytes 983048 | tf_op jit(solution)/shard_map/ppermute | solution.py:265
  51.2 0.1 fusion.2
  51.3 2.6 %collective-permute-start.5 = (bf16[2,2,80,512]{3,2,1,0:T(8,128)(2,1)S(1)}, bf16[2,2,80,512]{3,2,1,0:T(8,128)(2,1)S(1)}, u32[]{:S(2)}, u32[]{:S(2)}) collective-permute-start(bf16[2,2,80,512]{3,2,1,0:T(8,128)(2,1)S(1)} %get-tuple-element.33), channel_id=1, source_target_pairs={{0,7},{1,0},{2,1},{3,2},{4,3},{5,4},{6,5},{7,6},{8,15},{9,8},{10,9... | collective-permute-start | bytes 983048 | tf_op jit(solution)/shard_map/ppermute | solution.py:269
  53.9 2.8 %collective-permute-start.4 = (bf16[2,2,80,512]{3,2,1,0:T(8,128)(2,1)S(1)}, bf16[2,2,80,512]{3,2,1,0:T(8,128)(2,1)S(1)}, u32[]{:S(2)}, u32[]{:S(2)}) collective-permute-start(bf16[2,2,80,512]{3,2,1,0:T(8,128)(2,1)S(1)} %get-tuple-element.34), channel_id=1, source_target_pairs={{0,1},{1,2},{2,3},{3,4},{4,5},{5,6},{6,7},{7,0},{8,9},{9,10},{10,1... | collective-permute-start | bytes 983048 | tf_op jit(solution)/shard_map/ppermute | solution.py:268
  56.7 0.1 broadcast_subtract_fusion
  56.7 2.7 %collective-permute-done.5.high = bf16[2,2,80,512]{3,2,1,0:T(8,128)(2,1)S(1)} collective-permute-done((bf16[2,2,80,512]{3,2,1,0:T(8,128)(2,1)S(1)}, bf16[2,2,80,512]{3,2,1,0:T(8,128)(2,1)S(1)}, u32[]{:S(2)}, u32[]{:S(2)}) %collective-permute-start.5) | collective-permute-done | bytes 327712 | tf_op jit(solution)/shard_map/ppermute | solution.py:269
  59.5 3.4 %collective-permute-done.4.low = bf16[2,2,80,512]{3,2,1,0:T(8,128)(2,1)S(1)} collective-permute-done((bf16[2,2,80,512]{3,2,1,0:T(8,128)(2,1)S(1)}, bf16[2,2,80,512]{3,2,1,0:T(8,128)(2,1)S(1)}, u32[]{:S(2)}, u32[]{:S(2)}) %collective-permute-start.4) | collective-permute-done | bytes 327712 | tf_op jit(solution)/shard_map/ppermute | solution.py:268
  62.9 0.0 collective-permute-done.6.refs_2_
  62.9 1.7 shard_map.66
  64.6 13.5 %all_to_all.25 = bf16[4,4,2,32,512]{4,3,2,1,0:T(8,128)(2,1)S(1)} all-to-all(bf16[4,4,2,32,512]{4,3,2,1,0:T(8,128)(2,1)S(1)} %shard_map.66), channel_id=1, replica_groups=mesh['zh'=4,'zl'=4,'x'=4,'k'=2,'yh'=4,'yl'=2] {'x'}, dimensions={0} | all-to-all | bytes 2097152 | tf_op jit(solution)/shard_map/all_to_all | solution.py:186
  78.1 0.1 fusion
  78.2 30.3 %all_to_all.26 = bf16[4,2,32,512]{3,2,1,0:T(8,128)(2,1)S(1)} all-to-all(bf16[4,2,32,512]{3,2,1,0:T(8,128)(2,1)S(1)} %fusion), channel_id=1, replica_groups=mesh['zh'=4,'zl'=4,'x'=4,'k'=2,'yh'=4,'yl'=2] {'zh'}, dimensions={0} | all-to-all | bytes 524288 | tf_op jit(solution)/shard_map/all_to_all | solution.py:186
  108.6 18.6 %all_to_all.27 = bf16[4,2,32,512]{3,2,1,0:T(8,128)(2,1)S(1)} all-to-all(bf16[4,2,32,512]{3,2,1,0:T(8,128)(2,1)S(1)} %broadcast_in_dim.4), channel_id=1, replica_groups=mesh['zh'=4,'zl'=4,'x'=4,'k'=2,'yh'=4,'yl'=2] {'zh'}, dimensions={0} | all-to-all | bytes 524288 | tf_op jit(solution)/shard_map/all_to_all | solution.py:186
  127.2 0.1 broadcast_in_dim.5
  127.3 12.2 %all_to_all.28.amp_ref = bf16[4,4,2,32,512]{4,3,2,1,0:T(8,128)(2,1)S(1)} all-to-all(bf16[4,4,2,32,512]{4,3,2,1,0:T(8,128)(2,1)S(1)} %broadcast_in_dim.5), channel_id=1, replica_groups=mesh['zh'=4,'zl'=4,'x'=4,'k'=2,'yh'=4,'yl'=2] {'x'}, dimensions={0} | all-to-all | bytes 2097152 | tf_op jit(solution)/shard_map/all_to_all | solution.py:186
  139.4 1.4 shard_map.67
  140.8 14.6 %all_to_all.29.parts_ref = bf16[4,2,80,512]{3,2,1,0:T(8,128)(2,1)S(1)} all-to-all(bf16[4,2,80,512]{3,2,1,0:T(8,128)(2,1)S(1)} %shard_map.67), channel_id=1, replica_groups=mesh['zh'=4,'zl'=4,'x'=4,'k'=2,'yh'=4,'yl'=2] {'zl'}, dimensions={0} | all-to-all | bytes 1310720 | tf_op jit(solution)/shard_map/all_to_all | solution.py:186
  155.4 14.8 %collective-permute-start.7 = (f32[80,512]{1,0:T(8,128)S(1)}, f32[80,512]{1,0:T(8,128)S(1)}, u32[]{:S(2)}, u32[]{:S(2)}) collective-permute-start(f32[80,512]{1,0:T(8,128)S(1)} %add_bitcast_fusion), channel_id=1, source_target_pairs={{0,8},{8,0},{1,9},{9,1},{2,10},{10,2},{3,11},{11,3},{4,12},{12,4},... | collective-permute-start | bytes 491528 | tf_op jit(solution)/shard_map/ppermute | solution.py:282
  170.2 1.0 collective-permute-done.7.came_ref
  171.2 0.8 shard_map.68
  (6 shorter events, 0.2 us)
Async XLA Ops:
  5.0 21.8 %collective-permute-start = (bf16[80,512]{1,0:T(8,128)(2,1)}, bf16[80,512]{1,0:T(8,128)(2,1)S(1)}, u32[]{:S(2)}, u32[]{:S(2)}) collective-permute-start(bf16[80,512]{1,0:T(8,128)(2,1)} %get-tuple-element.19), channel_id=1, source_target_pairs={{0,0},{1,66},{2,132},{3,198},{4,8},{5,74},{6,140},{7,206},{8,1},{9... | collective-permute-start | bytes 245768 | tf_op jit(solution)/shard_map/ppermute | solution.py:246
  9.6 17.2 %collective-permute-start.1 = (bf16[80,512]{1,0:T(8,128)(2,1)}, bf16[80,512]{1,0:T(8,128)(2,1)S(1)}, u32[]{:S(2)}, u32[]{:S(2)}) collective-permute-start(bf16[80,512]{1,0:T(8,128)(2,1)} %get-tuple-element.20), channel_id=1, source_target_pairs={{0,8},{1,74},{2,140},{3,206},{4,0},{5,66},{6,132},{7,198},{8,9},{9... | collective-permute-start | bytes 245768 | tf_op jit(solution)/shard_map/ppermute | solution.py:246
  15.6 11.2 %collective-permute-start.2 = (bf16[80,512]{1,0:T(8,128)(2,1)}, bf16[80,512]{1,0:T(8,128)(2,1)S(1)}, u32[]{:S(2)}, u32[]{:S(2)}) collective-permute-start(bf16[80,512]{1,0:T(8,128)(2,1)} %get-tuple-element.22), channel_id=1, source_target_pairs={{0,8},{8,0},{1,9},{9,1},{2,10},{10,2},{3,11},{11,3},{4,12},{12,4},... | collective-permute-start | bytes 245768 | tf_op jit(solution)/shard_map/ppermute | solution.py:260
  26.8 0.9 copy-start
  27.7 19.7 %collective-permute-start.3 = (bf16[2,80,512]{2,1,0:T(8,128)(2,1)S(1)}, bf16[2,80,512]{2,1,0:T(8,128)(2,1)S(1)}, u32[]{:S(2)}, u32[]{:S(2)}) collective-permute-start(bf16[2,80,512]{2,1,0:T(8,128)(2,1)S(1)} %get-tuple-element.24.refs_0_), channel_id=1, source_target_pairs={{0,128},{64,192},{128,0},{192,64},{1,129},{65,193},{129,1},{193,65... | collective-permute-start | bytes 491528 | tf_op jit(solution)/shard_map/ppermute | solution.py:262
  47.5 15.4 %collective-permute-start.6 = (bf16[2,2,80,512]{3,2,1,0:T(8,128)(2,1)S(1)}, bf16[2,2,80,512]{3,2,1,0:T(8,128)(2,1)S(1)}, u32[]{:S(2)}, u32[]{:S(2)}) collective-permute-start(bf16[2,2,80,512]{3,2,1,0:T(8,128)(2,1)S(1)} %pad_maximum_fusion), channel_id=1, source_target_pairs={{0,64},{64,0},{128,192},{192,128},{1,65},{65,1},{129,193},{193,129... | collective-permute-start | bytes 983048 | tf_op jit(solution)/shard_map/ppermute | solution.py:265
  51.3 8.2 %collective-permute-start.5 = (bf16[2,2,80,512]{3,2,1,0:T(8,128)(2,1)S(1)}, bf16[2,2,80,512]{3,2,1,0:T(8,128)(2,1)S(1)}, u32[]{:S(2)}, u32[]{:S(2)}) collective-permute-start(bf16[2,2,80,512]{3,2,1,0:T(8,128)(2,1)S(1)} %get-tuple-element.33), channel_id=1, source_target_pairs={{0,7},{1,0},{2,1},{3,2},{4,3},{5,4},{6,5},{7,6},{8,15},{9,8},{10,9... | collective-permute-start | bytes 983048 | tf_op jit(solution)/shard_map/ppermute | solution.py:269
  53.9 9.0 %collective-permute-start.4 = (bf16[2,2,80,512]{3,2,1,0:T(8,128)(2,1)S(1)}, bf16[2,2,80,512]{3,2,1,0:T(8,128)(2,1)S(1)}, u32[]{:S(2)}, u32[]{:S(2)}) collective-permute-start(bf16[2,2,80,512]{3,2,1,0:T(8,128)(2,1)S(1)} %get-tuple-element.34), channel_id=1, source_target_pairs={{0,1},{1,2},{2,3},{3,4},{4,5},{5,6},{6,7},{7,0},{8,9},{9,10},{10,1... | collective-permute-start | bytes 983048 | tf_op jit(solution)/shard_map/ppermute | solution.py:268
  155.4 15.8 %collective-permute-start.7 = (f32[80,512]{1,0:T(8,128)S(1)}, f32[80,512]{1,0:T(8,128)S(1)}, u32[]{:S(2)}, u32[]{:S(2)}) collective-permute-start(f32[80,512]{1,0:T(8,128)S(1)} %add_bitcast_fusion), channel_id=1, source_target_pairs={{0,8},{8,0},{1,9},{9,1},{2,10},{10,2},{3,11},{11,3},{4,12},{12,4},... | collective-permute-start | bytes 491528 | tf_op jit(solution)/shard_map/ppermute | solution.py:282
